TPU v7x, 256 devices: a whole 4x4x8 slice. The times are simulated.
256 devices in a mesh: gx: 16 (over y_lo, x, core), gy: 16 (over y_hi, z).
Axes of the slice: x: 4, y: 4 (y_hi: 2, y_lo: 2; y = y_hi * 2 + y_lo), z: 8, core: 2. Of those that a mesh axis runs over, the one named last changes fastest.
Arguments:
- scalar_field: float32 [128, 8192], P('gx', 'gy'), may hold values from -6 to 6
- field_cotangent: float32 [128, 8192], P('gx', 'gy'), may hold values from -6 to 6
- diffusivity: float32 [128, 8192], P('gx', 'gy'), may hold values from 0.2 to 1
- velocity: float32 [3, 128, 8192], P(None, 'gx', 'gy'), may hold values from -3 to 3
- conv_in: bfloat16 [27, 32], replicated, may hold values from -1.25 to 1.25
- bias_in: float32 [32], replicated, may hold values from -3 to 3
- conv_mid: bfloat16 [27, 32, 32], replicated, may hold values from -0.21875 to 0.21875
- bias_mid: float32 [32], replicated, may hold values from -3 to 3
- flux_out: bfloat16 [32, 3], replicated, may hold values from -1 to 1
Outputs:
- grad_field: float32 [128, 8192], P('gx', 'gy')
- grad_conv_in: float32 [27, 32], replicated
- grad_bias_in: float32 [32], replicated
- grad_conv_mid: float32 [27, 32, 32], replicated
- grad_bias_mid: float32 [32], replicated
- grad_flux_out: float32 [32, 3], replicated
All inputs are finite; a program needn't handle non-finite values.
Results may differ from a plain program's by a relative error of at most 0.012.
The roundings to bfloat16 on the way count: a program that leaves them out, or rounds other values in their place, can miss the bound.
Values may be sent and summed in bfloat16 or wider, within the bound.
A program may use at most 64 MiB of HBM per device.

v0:
```python
import math

import jax
import jax.numpy as jnp
from jax import lax
from jax.sharding import PartitionSpec as P

NZ = 32


time_step = 0.2
highest = lax.Precision.HIGHEST


def extended(value, sides, width):
    for axis, dim in sides:
        size, length = (lax.axis_size(axis), value.shape[dim])
        up = [(i, (i + 1) % size) for i in range(size)]
        down = [(j, i) for i, j in up]
        last = lax.slice_in_dim(value, length - width, length, axis=dim)
        leading = lax.slice_in_dim(value, 0, width, axis=dim)
        before = lax.ppermute(last, axis, up)
        after = lax.ppermute(leading, axis, down)
        value = jnp.concatenate([before, value, after], axis=dim)
    return value


def offsets():
    return [
        (step_x, step_y, step_z)
        for step_x in (-1, 0, 1)
        for step_y in (-1, 0, 1)
        for step_z in (-1, 0, 1)
    ]


def window(values, step_x, step_y):
    row_count = values.shape[-2]
    col_count = values.shape[-1]
    return values[
        ..., 1 + step_x : row_count - 1 + step_x, (1 + step_y) * NZ : col_count - (1 - step_y) * NZ
    ]


def crop(values, margin):
    row_count = values.shape[-2]
    col_count = values.shape[-1]
    return values[..., margin : row_count - margin, margin * NZ : col_count - margin * NZ]


def lift(values, step_z):
    if step_z == 0:
        return values
    length_z = values.shape[-1]
    padded = jnp.pad(values, [(0, 0)] * (values.ndim - 1) + [(1, 1)])
    shifted = lax.slice_in_dim(padded, 1 + step_z, 1 + step_z + length_z, axis=values.ndim - 1)
    plane_index = lax.broadcasted_iota(jnp.int32, (length_z,), 0) % NZ + step_z
    inside = (plane_index >= 0) & (plane_index < NZ)
    return jnp.where(inside, shifted, jnp.zeros_like(shifted))


def central_ext(values, dimension):
    if dimension == 0:
        return 0.5 * (window(values, 1, 0) - window(values, -1, 0))
    if dimension == 1:
        return 0.5 * (window(values, 0, 1) - window(values, 0, -1))
    centre = window(values, 0, 0)
    return 0.5 * (lift(centre, 1) - lift(centre, -1))


def laplace_ext(values):
    centre = window(values, 0, 0)
    running = (
        window(values, 1, 0) + window(values, -1, 0) + window(values, 0, 1) + window(values, 0, -1)
    )
    return running + lift(centre, 1) + lift(centre, -1) - 6.0 * centre


def to_blocks(values):
    return values.reshape(values.shape[:-1] + (values.shape[-1] // NZ, NZ))


def from_blocks(values):
    return values.reshape(values.shape[:-2] + (values.shape[-2] * NZ,))


def conv_first(rounded, conv_in):
    weights = conv_in.astype(jnp.float32)
    running = 0.0
    for plane_step in (-1, 0, 1):
        partial_sum = 0.0
        for number, offset in enumerate(offsets()):
            if offset[2] == plane_step:
                partial_sum = (
                    partial_sum
                    + weights[number][:, None, None]
                    * window(rounded, offset[0], offset[1]).astype(jnp.float32)[None]
                )
        running = running + lift(partial_sum, plane_step)
    return running


def conv_middle(hidden, conv_mid):
    running = 0.0
    for plane_step in (-1, 0, 1):
        partial_sum = 0.0
        for number, offset in enumerate(offsets()):
            if offset[2] == plane_step:
                partial_sum = partial_sum + jnp.einsum(
                    "cxn,co->oxn",
                    window(hidden, offset[0], offset[1]),
                    conv_mid[number],
                    preferred_element_type=jnp.float32,
                )
        running = running + lift(partial_sum, plane_step)
    return running


def conv_middle_back(gradient, conv_mid):
    running = 0.0
    for plane_step in (-1, 0, 1):
        partial_sum = 0.0
        for number, offset in enumerate(offsets()):
            if offset[2] == plane_step:
                partial_sum = partial_sum + jnp.einsum(
                    "oxn,co->cxn",
                    window(gradient, -offset[0], -offset[1]),
                    conv_mid[number],
                    preferred_element_type=jnp.float32,
                )
        running = running + lift(partial_sum, -plane_step)
    return running


def conv_first_back(gradient, conv_in):
    running = 0.0
    for plane_step in (-1, 0, 1):
        partial_sum = 0.0
        for number, offset in enumerate(offsets()):
            if offset[2] == plane_step:
                partial_sum = partial_sum + jnp.einsum(
                    "cxn,c->xn",
                    window(gradient, -offset[0], -offset[1]),
                    conv_in[number],
                    preferred_element_type=jnp.float32,
                )
        running = running + lift(partial_sum, -plane_step)
    return running


def advance(current, diffusivity, velocity, params, needed):
    conv_in, bias_in, conv_mid, bias_mid, flux_out = params
    inner_rows = current.shape[0]
    near_field = from_blocks(extended(to_blocks(current[None]), (("gx", 1), ("gy", 2)), 1))[0]
    rounded = near_field.astype(jnp.bfloat16)
    hidden_core = jnp.tanh(conv_first(rounded, conv_in) + bias_in[:, None, None]).astype(
        jnp.bfloat16
    )
    hidden_one = from_blocks(extended(to_blocks(hidden_core), (("gx", 1), ("gy", 2)), 2))
    hidden_two = jnp.tanh(conv_middle(hidden_one, conv_mid) + bias_mid[:, None, None]).astype(
        jnp.bfloat16
    )
    stored = (rounded, hidden_one, hidden_two)
    if not needed:
        return (current, stored)
    fluxes = jnp.einsum("cxn,cd->dxn", hidden_two, flux_out, preferred_element_type=jnp.float32)
    correction = central_ext(fluxes[0], 0) + central_ext(fluxes[1], 1) + central_ext(fluxes[2], 2)
    correction = crop(correction, (correction.shape[-2] - inner_rows) // 2)
    physics = diffusivity * laplace_ext(near_field)
    for dimension in range(3):
        physics = physics - velocity[dimension] * central_ext(near_field, dimension)
    return (current + time_step * (physics + correction), stored)


def retreat(adjoint, stored, diffusivity, velocity, params):
    conv_in, bias_in, conv_mid, bias_mid, flux_out = params
    rounded, hidden_one, hidden_two = stored
    inner_rows = adjoint.shape[0]
    margin = (hidden_two.shape[-2] - inner_rows) // 2
    stacked = jnp.stack(
        [
            adjoint,
            diffusivity * adjoint,
            velocity[0] * adjoint,
            velocity[1] * adjoint,
            velocity[2] * adjoint,
        ]
    )
    spread = from_blocks(extended(to_blocks(stacked), (("gx", 1), ("gy", 2)), 2))
    grad_flux = jnp.stack(
        [-time_step * central_ext(spread[0], dimension) for dimension in range(3)]
    )
    two_wide = hidden_two.astype(jnp.float32)
    term_out = jnp.einsum(
        "cxn,dxn->cd", crop(two_wide, margin), crop(grad_flux, margin), precision=highest
    )
    back_two = jnp.einsum("cd,dxn->cxn", flux_out.astype(jnp.float32), grad_flux, precision=highest)
    grad_two = (back_two * (1.0 - two_wide * two_wide)).astype(jnp.bfloat16)
    grad_two_inner = crop(grad_two, margin)
    term_bias_mid = jnp.sum(grad_two_inner.astype(jnp.float32), axis=(1, 2))
    hidden_near = crop(hidden_one, (hidden_one.shape[-2] - inner_rows) // 2 - 1)
    term_mid = jnp.stack(
        [
            jnp.einsum(
                "cxn,oxn->co",
                lift(window(hidden_near, offset[0], offset[1]), offset[2]),
                grad_two_inner,
                preferred_element_type=jnp.float32,
            )
            for offset in offsets()
        ]
    )
    back_one = conv_middle_back(grad_two, conv_mid)
    hidden_match = crop(hidden_one, (hidden_one.shape[-2] - back_one.shape[-2]) // 2).astype(
        jnp.float32
    )
    grad_one = (back_one * (1.0 - hidden_match * hidden_match)).astype(jnp.bfloat16)
    grad_near = from_blocks(extended(to_blocks(grad_one), (("gx", 1), ("gy", 2)), 1))
    grad_one_inner = crop(grad_near, 1)
    term_bias_in = jnp.sum(grad_one_inner.astype(jnp.float32), axis=(1, 2))
    rounded_near = crop(rounded, (rounded.shape[-2] - inner_rows) // 2 - 1)
    term_in = jnp.stack(
        [
            jnp.einsum(
                "xn,cxn->c",
                lift(window(rounded_near, offset[0], offset[1]), offset[2]),
                grad_one_inner,
                preferred_element_type=jnp.float32,
            )
            for offset in offsets()
        ]
    )
    back_field = conv_first_back(grad_near, conv_in)
    near_stack = crop(spread, (spread.shape[-2] - inner_rows) // 2 - 1)
    physics = laplace_ext(near_stack[1])
    for dimension in range(3):
        physics = physics + central_ext(near_stack[2 + dimension], dimension)
    previous = adjoint + time_step * physics + back_field
    return (previous, (term_in, term_bias_in, term_mid, term_bias_mid, term_out))


def shards(
    scalar_field,
    field_cotangent,
    diffusivity,
    velocity,
    conv_in,
    bias_in,
    conv_mid,
    bias_mid,
    flux_out,
):
    params = (conv_in, bias_in, conv_mid, bias_mid, flux_out)
    field_one, stored_one = advance(scalar_field, diffusivity, velocity, params, True)
    stored_two = advance(field_one, diffusivity, velocity, params, False)[1]
    adjoint_one, terms_two = retreat(field_cotangent, stored_two, diffusivity, velocity, params)
    adjoint_zero, terms_one = retreat(adjoint_one, stored_one, diffusivity, velocity, params)
    joined = tuple((first + second for first, second in zip(terms_one, terms_two)))
    totals = lax.psum((joined[0], joined[1], joined[2], joined[3], joined[4]), ("gx", "gy"))
    cells = (
        scalar_field.shape[0] * lax.axis_size("gx") * scalar_field.shape[1] * lax.axis_size("gy")
    )
    scale = 1.0 / math.sqrt(cells)
    return (
        adjoint_zero,
        totals[0] * scale,
        totals[1] * scale,
        totals[2] * scale,
        totals[3] * scale,
        totals[4] * scale,
    )


def solution(mesh):
    return jax.shard_map(
        shards,
        mesh=mesh,
        in_specs=(
            P("gx", "gy"),
            P("gx", "gy"),
            P("gx", "gy"),
            P(None, "gx", "gy"),
            P(),
            P(),
            P(),
            P(),
            P(),
        ),
        out_specs=(P("gx", "gy"), P(), P(), P(), P(), P()),
        check_vma=False,
    )
```

profile of v0, /device:TPU:1, one launch (start us, length us, event | category | flops | bytes accessed | tf_op | source)
XLA Modules:
  0.0 462.2 jit_solution(14635057262695785889)
XLA Ops:
  7.2 0.8 reshape_broadcast_in_dim.6
  8.1 2.7 collective-permute-start.4
  10.7 0.7 collective-permute-start.5
  11.5 0.8 stack.396
  12.3 0.8 bitcast_multiply_fusion.2
  13.5 1.1 collective-permute-start
  14.6 2.8 collective-permute-start.1
  18.5 6.5 %collective-permute-start.7 = (f32[1,10,1,32]{3,2,1,0:T(1,128)S(1)}, f32[1,10,1,32]{3,2,1,0:T(1,128)S(1)}, u32[]{:S(2)}, u32[]{:S(2)}) collective-permute-start(f32[1,10,1,32]{3,2,1,0:T(1,128)S(1)} %get-tuple-element.66), channel_id=1, source_target_pairs={{1,0},{2,1},{3,2},{4,3},{5,4},{6,5},{7,6},{8,7},{9,8},{10,9},{11,1... | collective-permute-start | bytes 3848 | tf_op jit(solution)/shard_map/ppermute | solution.py:23
  25.0 0.9 collective-permute-done.6
  29.1 0.7 fusion.1282
  30.5 1.5 collective-permute-start.8
  32.1 3.2 collective-permute-start.9
  35.4 5.5 %collective-permute-start.3 = (f32[5,12,2,32]{3,2,1,0:T(2,128)S(1)}, f32[5,12,2,32]{3,2,1,0:T(2,128)S(1)}, u32[]{:S(2)}, u32[]{:S(2)}) collective-permute-start(f32[5,12,2,32]{3,2,1,0:T(2,128)S(1)} %get-tuple-element.49), channel_id=1, source_target_pairs={{1,0},{2,1},{3,2},{4,3},{5,4},{6,5},{7,6},{8,7},{9,8},{10,9},{11,1... | collective-permute-start | bytes 46088 | tf_op jit(solution)/shard_map/ppermute | solution.py:23
  41.7 1.4 collective-permute-done.2
  43.5 0.8 slice_bitcast_fusion.7
  45.4 5.2 %collective-permute-start.11 = (bf16[32,12,2,32]{3,2,0,1:T(2,128)(2,1)S(1)}, bf16[32,12,2,32]{3,2,0,1:T(2,128)(2,1)S(1)}, u32[]{:S(2)}, u32[]{:S(2)}) collective-permute-start(bf16[32,12,2,32]{3,2,0,1:T(2,128)(2,1)S(1)} %get-tuple-element.15), channel_id=1, source_target_pairs={{1,0},{2,1},{3,2},{4,3},{5,4},{6,5},{7,6},{8,7},{9,8},{10,9},{11,1... | collective-permute-start | bytes 147464 | tf_op jit(solution)/shard_map/ppermute | solution.py:23
  51.3 2.3 collective-permute-done.10
  53.6 1.3 pad_maximum_fusion
  54.9 1.3 reshape.118
  65.4 0.8 fusion.58
  66.1 0.7 copy-done.3
  70.1 1.5 slice.1907
  71.5 5.1 %collective-permute-start.13 = (bf16[1,1,16,32]{3,2,1,0:T(8,128)(2,1)S(1)}, bf16[1,1,16,32]{3,2,1,0:T(8,128)(2,1)S(1)}, u32[]{:S(2)}, u32[]{:S(2)}) collective-permute-start(bf16[1,1,16,32]{3,2,1,0:T(8,128)(2,1)S(1)} %get-tuple-element.82), channel_id=1, source_target_pairs={{16,0},{32,16},{48,32},{64,48},{80,64},{96,80},{112,96},{128,112},... | collective-permute-start | bytes 3080 | tf_op jit(solution)/shard_map/ppermute | solution.py:23
  76.6 0.8 collective-permute-done.13
  77.8 5.5 %collective-permute-start.15 = (bf16[1,10,1,32]{3,2,1,0:T(2,128)(2,1)S(1)}, bf16[1,10,1,32]{3,2,1,0:T(2,128)(2,1)S(1)}, u32[]{:S(2)}, u32[]{:S(2)}) collective-permute-start(bf16[1,10,1,32]{3,2,1,0:T(2,128)(2,1)S(1)} %get-tuple-element.81), channel_id=1, source_target_pairs={{1,0},{2,1},{3,2},{4,3},{5,4},{6,5},{7,6},{8,7},{9,8},{10,9},{11,1... | collective-permute-start | bytes 1928 | tf_op jit(solution)/shard_map/ppermute | solution.py:23
  83.3 2.2 fusion.1284
  85.7 0.7 slice_bitcast_fusion.35
  89.0 4.7 %collective-permute-start.17 = (bf16[32,2,16,32]{3,2,0,1:T(8,128)(2,1)S(1)}, bf16[32,2,16,32]{3,2,0,1:T(8,128)(2,1)S(1)}, u32[]{:S(2)}, u32[]{:S(2)}) collective-permute-start(bf16[32,2,16,32]{3,2,0,1:T(8,128)(2,1)S(1)} %get-tuple-element.24), channel_id=1, source_target_pairs={{16,0},{32,16},{48,32},{64,48},{80,64},{96,80},{112,96},{128,112},... | collective-permute-start | bytes 196616 | tf_op jit(solution)/shard_map/ppermute | solution.py:23
  93.7 0.8 fusion.680
  95.5 5.1 %collective-permute-start.19 = (bf16[32,12,2,32]{3,2,0,1:T(2,128)(2,1)S(1)}, bf16[32,12,2,32]{3,2,0,1:T(2,128)(2,1)S(1)}, u32[]{:S(2)}, u32[]{:S(2)}) collective-permute-start(bf16[32,12,2,32]{3,2,0,1:T(2,128)(2,1)S(1)} %get-tuple-element.13), channel_id=1, source_target_pairs={{1,0},{2,1},{3,2},{4,3},{5,4},{6,5},{7,6},{8,7},{9,8},{10,9},{11,1... | collective-permute-start | bytes 147464 | tf_op jit(solution)/shard_map/ppermute | solution.py:23
  100.6 0.8 fusion.684
  101.4 2.2 collective-permute-done.18
  103.6 1.3 pad_maximum_fusion.1
  104.9 1.5 reshape.120
  106.5 1.1 fusion.149
  107.6 1.0 fusion.155
  115.8 0.8 fusion.1283
  117.8 0.8 fusion.59
  123.7 0.7 fusion.92
  136.7 1.4 collective-permute-start.20
  138.1 0.9 fusion.76
  139.0 7.6 %collective-permute-start.21 = (bf16[32,1,16,32]{3,2,0,1:T(8,128)(2,1)S(1)}, bf16[32,1,16,32]{3,2,0,1:T(8,128)(2,1)S(1)}, u32[]{:S(2)}, u32[]{:S(2)}) collective-permute-start(bf16[32,1,16,32]{3,2,0,1:T(8,128)(2,1)S(1)} %get-tuple-element.22), channel_id=1, source_target_pairs={{16,0},{32,16},{48,32},{64,48},{80,64},{96,80},{112,96},{128,112},... | collective-permute-start | bytes 98312 | tf_op jit(solution)/shard_map/ppermute | solution.py:23
  148.1 5.6 %collective-permute-start.23 = (bf16[32,10,1,32]{3,2,0,1:T(2,128)(2,1)S(1)}, bf16[32,10,1,32]{3,2,0,1:T(2,128)(2,1)S(1)}, u32[]{:S(2)}, u32[]{:S(2)}) collective-permute-start(bf16[32,10,1,32]{3,2,0,1:T(2,128)(2,1)S(1)} %get-tuple-element.19), channel_id=1, source_target_pairs={{1,0},{2,1},{3,2},{4,3},{5,4},{6,5},{7,6},{8,7},{9,8},{10,9},{11,1... | collective-permute-start | bytes 61448 | tf_op jit(solution)/shard_map/ppermute | solution.py:23
  153.7 0.8 convert_reduce_fusion
  154.5 1.7 collective-permute-done.22
  156.2 1.1 pad_maximum_fusion.2
  157.3 1.1 reshape.122
  164.7 0.8 convert_reduce_fusion.2
  166.0 6.3 %collective-permute-start.25 = (f32[5,2,16,32]{3,2,1,0:T(8,128)S(1)}, f32[5,2,16,32]{3,2,1,0:T(8,128)S(1)}, u32[]{:S(2)}, u32[]{:S(2)}) collective-permute-start(f32[5,2,16,32]{3,2,1,0:T(8,128)S(1)} %get-tuple-element.51), channel_id=1, source_target_pairs={{16,0},{32,16},{48,32},{64,48},{80,64},{96,80},{112,96},{128,112},... | collective-permute-start | bytes 61448 | tf_op jit(solution)/shard_map/ppermute | solution.py:23
  179.9 5.7 %collective-permute-start.27 = (f32[5,12,2,32]{3,2,1,0:T(2,128)S(1)}, f32[5,12,2,32]{3,2,1,0:T(2,128)S(1)}, u32[]{:S(2)}, u32[]{:S(2)}) collective-permute-start(f32[5,12,2,32]{3,2,1,0:T(2,128)S(1)} %get-tuple-element.47), channel_id=1, source_target_pairs={{1,0},{2,1},{3,2},{4,3},{5,4},{6,5},{7,6},{8,7},{9,8},{10,9},{11,1... | collective-permute-start | bytes 46088 | tf_op jit(solution)/shard_map/ppermute | solution.py:23
  185.9 1.2 collective-permute-done.26
  188.5 1.1 fusion.434
  189.6 1.1 fusion.430
  200.4 0.8 add.1959
  201.6 1.3 convolution_add_fusion.13
  211.3 4.7 %collective-permute-start.29 = (bf16[32,1,16,32]{3,2,0,1:T(8,128)(2,1)S(1)}, bf16[32,1,16,32]{3,2,0,1:T(8,128)(2,1)S(1)}, u32[]{:S(2)}, u32[]{:S(2)}) collective-permute-start(bf16[32,1,16,32]{3,2,0,1:T(8,128)(2,1)S(1)} %get-tuple-element.20), channel_id=1, source_target_pairs={{16,0},{32,16},{48,32},{64,48},{80,64},{96,80},{112,96},{128,112},... | collective-permute-start | bytes 98312 | tf_op jit(solution)/shard_map/ppermute | solution.py:23
  217.4 5.5 %collective-permute-start.31 = (bf16[32,10,1,32]{3,2,0,1:T(2,128)(2,1)S(1)}, bf16[32,10,1,32]{3,2,0,1:T(2,128)(2,1)S(1)}, u32[]{:S(2)}, u32[]{:S(2)}) collective-permute-start(bf16[32,10,1,32]{3,2,0,1:T(2,128)(2,1)S(1)} %get-tuple-element.17), channel_id=1, source_target_pairs={{1,0},{2,1},{3,2},{4,3},{5,4},{6,5},{7,6},{8,7},{9,8},{10,9},{11,1... | collective-permute-start | bytes 61448 | tf_op jit(solution)/shard_map/ppermute | solution.py:23
  223.7 1.9 collective-permute-done.30
  225.6 1.1 pad_maximum_fusion.3
  226.8 1.1 reshape.125
  241.5 85.2 %all-reduce.60 = (f32[27,32]{1,0:T(8,128)S(1)}, f32[32]{0:T(128)S(1)}, f32[32]{0:T(128)S(1)}, f32[32,3]{0,1:T(4,128)S(1)}) all-reduce(f32[27,32]{1,0:T(8,128)S(1)} %add.1957, f32[32]{0:T(128)S(1)} %add.1958, f32[32]{0:T(128)S(1)} %copy-done.167, f32[32,3]{0,1:T(4,128)S(1)} %fusion.130), channel_id=1, replica_groups=mesh['gx'=16,'gy'=16] {'gx','gy'}, use_global_device_ids=true, to_apply=%region_0.1 | all-reduce | flops 1024 | bytes 8192 | tf_op jit(solution)/shard_map/psum | solution.py:259
  328.4 0.7 fusion.575
  329.6 123.7 %all-reduce.63.cloned.1.call-done = f32[27,32,32]{2,1,0:T(8,128)} async-done(((f32[27,32,32]{2,1,0:T(8,128)}), f32[27,32,32]{2,1,0:T(8,128)}) %all-reduce.63.cloned.1.call-update) | async-done | bytes 110608 | tf_op jit(solution)/shard_map/psum | solution.py:259
  453.3 1.8 broadcast_multiply_fusion
  (761 shorter events, 102.3 us)
Async XLA Ops:
  7.2 59.7 %copy-start = (bf16[32,3]{0,1:T(4,128)(2,1)S(1)}, bf16[32,3]{0,1:T(4,128)(2,1)}, u32[]{:S(2)}) copy-start(bf16[32,3]{0,1:T(4,128)(2,1)} %param.17) | copy-start | bytes 580
  7.2 446.1 %all-reduce.63.cloned.1.call-start = ((), (), s32[]{:S(2)}) async-start(), calls=%async_computation | async-start | bytes 884736 | tf_op jit(solution)/shard_map/psum | solution.py:259
  8.1 10.3 %collective-permute-start.4 = (f32[1,1,16,32]{3,2,1,0:T(8,128)S(1)}, f32[1,1,16,32]{3,2,1,0:T(8,128)S(1)}, u32[]{:S(2)}, u32[]{:S(2)}) collective-permute-start(f32[1,1,16,32]{3,2,1,0:T(8,128)S(1)} %get-tuple-element.73), channel_id=1, source_target_pairs={{0,16},{16,32},{32,48},{48,64},{64,80},{80,96},{96,112},{112,128},... | collective-permute-start | bytes 6152 | tf_op jit(solution)/shard_map/ppermute | solution.py:22
  10.7 7.6 %collective-permute-start.5 = (f32[1,1,16,32]{3,2,1,0:T(8,128)S(1)}, f32[1,1,16,32]{3,2,1,0:T(8,128)S(1)}, u32[]{:S(2)}, u32[]{:S(2)}) collective-permute-start(f32[1,1,16,32]{3,2,1,0:T(8,128)S(1)} %get-tuple-element.72), channel_id=1, source_target_pairs={{16,0},{32,16},{48,32},{64,48},{80,64},{96,80},{112,96},{128,112},... | collective-permute-start | bytes 6152 | tf_op jit(solution)/shard_map/ppermute | solution.py:23
  13.4 14.2 %copy-start.161 = (f32[32]{0:T(128)S(1)}, f32[32]{0:T(128)}, u32[]{:S(2)}) copy-start(f32[32]{0:T(128)} %param.14) | copy-start | bytes 388
  13.5 21.8 %collective-permute-start = (f32[5,2,16,32]{3,2,1,0:T(8,128)S(1)}, f32[5,2,16,32]{3,2,1,0:T(8,128)S(1)}, u32[]{:S(2)}, u32[]{:S(2)}) collective-permute-start(f32[5,2,16,32]{3,2,1,0:T(8,128)S(1)} %get-tuple-element.52), channel_id=1, source_target_pairs={{0,16},{16,32},{32,48},{48,64},{64,80},{80,96},{96,112},{112,128},... | collective-permute-start | bytes 61448 | tf_op jit(solution)/shard_map/ppermute | solution.py:22
  14.6 20.7 %collective-permute-start.1 = (f32[5,2,16,32]{3,2,1,0:T(8,128)S(1)}, f32[5,2,16,32]{3,2,1,0:T(8,128)S(1)}, u32[]{:S(2)}, u32[]{:S(2)}) collective-permute-start(f32[5,2,16,32]{3,2,1,0:T(8,128)S(1)} %get-tuple-element.53), channel_id=1, source_target_pairs={{16,0},{32,16},{48,32},{64,48},{80,64},{96,80},{112,96},{128,112},... | collective-permute-start | bytes 61448 | tf_op jit(solution)/shard_map/ppermute | solution.py:23
  17.4 10.8 %copy-start.107 = (f32[32]{0:T(128)}, f32[32]{0:T(128)S(1)}, u32[]{:S(2)}) copy-start(f32[32]{0:T(128)S(1)} %get-tuple-element.140) | copy-start | bytes 388
  17.4 10.8 %copy-start.109 = (f32[32]{0:T(128)}, f32[32]{0:T(128)S(1)}, u32[]{:S(2)}) copy-start(f32[32]{0:T(128)S(1)} %get-tuple-element.150) | copy-start | bytes 388
  17.4 10.8 %copy-start.111 = (f32[32]{0:T(128)}, f32[32]{0:T(128)S(1)}, u32[]{:S(2)}) copy-start(f32[32]{0:T(128)S(1)} %get-tuple-element.151) | copy-start | bytes 388
  17.5 10.8 %copy-start.113 = (f32[32]{0:T(128)}, f32[32]{0:T(128)S(1)}, u32[]{:S(2)}) copy-start(f32[32]{0:T(128)S(1)} %get-tuple-element.152) | copy-start | bytes 388
  17.5 10.8 %copy-start.115 = (f32[32]{0:T(128)}, f32[32]{0:T(128)S(1)}, u32[]{:S(2)}) copy-start(f32[32]{0:T(128)S(1)} %get-tuple-element.153) | copy-start | bytes 388
  17.5 10.8 %copy-start.117 = (f32[32]{0:T(128)}, f32[32]{0:T(128)S(1)}, u32[]{:S(2)}) copy-start(f32[32]{0:T(128)S(1)} %get-tuple-element.154) | copy-start | bytes 388
  17.5 10.8 %copy-start.119 = (f32[32]{0:T(128)}, f32[32]{0:T(128)S(1)}, u32[]{:S(2)}) copy-start(f32[32]{0:T(128)S(1)} %get-tuple-element.155) | copy-start | bytes 388
  17.5 10.8 %copy-start.121 = (f32[32]{0:T(128)}, f32[32]{0:T(128)S(1)}, u32[]{:S(2)}) copy-start(f32[32]{0:T(128)S(1)} %get-tuple-element.156) | copy-start | bytes 388
  17.5 10.8 %copy-start.123 = (f32[32]{0:T(128)}, f32[32]{0:T(128)S(1)}, u32[]{:S(2)}) copy-start(f32[32]{0:T(128)S(1)} %get-tuple-element.157) | copy-start | bytes 388
  17.5 10.8 %copy-start.125 = (f32[32]{0:T(128)}, f32[32]{0:T(128)S(1)}, u32[]{:S(2)}) copy-start(f32[32]{0:T(128)S(1)} %get-tuple-element.158) | copy-start | bytes 388
  17.5 10.8 %copy-start.127 = (f32[32]{0:T(128)}, f32[32]{0:T(128)S(1)}, u32[]{:S(2)}) copy-start(f32[32]{0:T(128)S(1)} %get-tuple-element.141) | copy-start | bytes 388
  17.5 10.8 %copy-start.129 = (f32[32]{0:T(128)}, f32[32]{0:T(128)S(1)}, u32[]{:S(2)}) copy-start(f32[32]{0:T(128)S(1)} %get-tuple-element.142) | copy-start | bytes 388
  17.6 10.8 %copy-start.131 = (f32[32]{0:T(128)}, f32[32]{0:T(128)S(1)}, u32[]{:S(2)}) copy-start(f32[32]{0:T(128)S(1)} %get-tuple-element.143) | copy-start | bytes 388
  17.6 10.8 %copy-start.133 = (f32[32]{0:T(128)}, f32[32]{0:T(128)S(1)}, u32[]{:S(2)}) copy-start(f32[32]{0:T(128)S(1)} %get-tuple-element.144) | copy-start | bytes 388
  17.6 10.8 %copy-start.135 = (f32[32]{0:T(128)}, f32[32]{0:T(128)S(1)}, u32[]{:S(2)}) copy-start(f32[32]{0:T(128)S(1)} %get-tuple-element.145) | copy-start | bytes 388
  17.6 10.8 %copy-start.137 = (f32[32]{0:T(128)}, f32[32]{0:T(128)S(1)}, u32[]{:S(2)}) copy-start(f32[32]{0:T(128)S(1)} %get-tuple-element.146) | copy-start | bytes 388
  17.6 10.8 %copy-start.139 = (f32[32]{0:T(128)}, f32[32]{0:T(128)S(1)}, u32[]{:S(2)}) copy-start(f32[32]{0:T(128)S(1)} %get-tuple-element.147) | copy-start | bytes 388
  17.6 10.8 %copy-start.141 = (f32[32]{0:T(128)}, f32[32]{0:T(128)S(1)}, u32[]{:S(2)}) copy-start(f32[32]{0:T(128)S(1)} %get-tuple-element.148) | copy-start | bytes 388
  17.6 10.8 %copy-start.143 = (f32[32]{0:T(128)}, f32[32]{0:T(128)S(1)}, u32[]{:S(2)}) copy-start(f32[32]{0:T(128)S(1)} %get-tuple-element.149) | copy-start | bytes 388
  17.6 10.8 %copy-start.145 = (f32[32]{0:T(128)}, f32[32]{0:T(128)S(1)}, u32[]{:S(2)}) copy-start(f32[32]{0:T(128)S(1)} %get-tuple-element.159) | copy-start | bytes 388
  17.6 10.8 %copy-start.147 = (f32[32]{0:T(128)}, f32[32]{0:T(128)S(1)}, u32[]{:S(2)}) copy-start(f32[32]{0:T(128)S(1)} %get-tuple-element.160) | copy-start | bytes 388
  17.7 10.8 %copy-start.149 = (f32[32]{0:T(128)}, f32[32]{0:T(128)S(1)}, u32[]{:S(2)}) copy-start(f32[32]{0:T(128)S(1)} %get-tuple-element.161) | copy-start | bytes 388
  17.7 10.8 %copy-start.151 = (f32[32]{0:T(128)}, f32[32]{0:T(128)S(1)}, u32[]{:S(2)}) copy-start(f32[32]{0:T(128)S(1)} %get-tuple-element.162) | copy-start | bytes 388
  17.7 10.8 %copy-start.153 = (f32[32]{0:T(128)}, f32[32]{0:T(128)S(1)}, u32[]{:S(2)}) copy-start(f32[32]{0:T(128)S(1)} %get-tuple-element.163) | copy-start | bytes 388
  17.7 10.8 %copy-start.155 = (f32[32]{0:T(128)}, f32[32]{0:T(128)S(1)}, u32[]{:S(2)}) copy-start(f32[32]{0:T(128)S(1)} %get-tuple-element.164) | copy-start | bytes 388
  17.7 10.8 %copy-start.157 = (f32[32]{0:T(128)}, f32[32]{0:T(128)S(1)}, u32[]{:S(2)}) copy-start(f32[32]{0:T(128)S(1)} %get-tuple-element.165) | copy-start | bytes 388
  17.7 10.8 %copy-start.159 = (f32[32]{0:T(128)}, f32[32]{0:T(128)S(1)}, u32[]{:S(2)}) copy-start(f32[32]{0:T(128)S(1)} %get-tuple-element.166) | copy-start | bytes 388
  18.4 7.6 %collective-permute-start.6 = (f32[1,10,1,32]{3,2,1,0:T(1,128)S(1)}, f32[1,10,1,32]{3,2,1,0:T(1,128)S(1)}, u32[]{:S(2)}, u32[]{:S(2)}) collective-permute-start(f32[1,10,1,32]{3,2,1,0:T(1,128)S(1)} %get-tuple-element.65), channel_id=1, source_target_pairs={{0,1},{1,2},{2,3},{3,4},{4,5},{5,6},{6,7},{7,8},{8,9},{9,10},{10,1... | collective-permute-start | bytes 3848 | tf_op jit(solution)/shard_map/ppermute | solution.py:22
  18.5 7.5 %collective-permute-start.7 = (f32[1,10,1,32]{3,2,1,0:T(1,128)S(1)}, f32[1,10,1,32]{3,2,1,0:T(1,128)S(1)}, u32[]{:S(2)}, u32[]{:S(2)}) collective-permute-start(f32[1,10,1,32]{3,2,1,0:T(1,128)S(1)} %get-tuple-element.66), channel_id=1, source_target_pairs={{1,0},{2,1},{3,2},{4,3},{5,4},{6,5},{7,6},{8,7},{9,8},{10,9},{11,1... | collective-permute-start | bytes 3848 | tf_op jit(solution)/shard_map/ppermute | solution.py:23
  25.0 15.9 %copy-start.29 = (pred[512]{0:T(512)(128)(4,1)}, pred[512]{0:T(512)(128)(4,1)S(1)}, u32[]{:S(2)}) copy-start(pred[512]{0:T(512)(128)(4,1)S(1)} %get-tuple-element.234) | copy-start | bytes 1540
  30.5 13.8 %collective-permute-start.8 = (bf16[32,2,16,32]{3,2,0,1:T(8,128)(2,1)}, bf16[32,2,16,32]{3,2,0,1:T(8,128)(2,1)S(1)}, u32[]{:S(2)}, u32[]{:S(2)}) collective-permute-start(bf16[32,2,16,32]{3,2,0,1:T(8,128)(2,1)} %get-tuple-element.27), channel_id=1, source_target_pairs={{0,16},{16,32},{32,48},{48,64},{64,80},{80,96},{96,112},{112,128},... | collective-permute-start | bytes 196616 | tf_op jit(solution)/shard_map/ppermute | solution.py:22
  32.1 12.6 %collective-permute-start.9 = (bf16[32,2,16,32]{3,2,0,1:T(8,128)(2,1)S(1)}, bf16[32,2,16,32]{3,2,0,1:T(8,128)(2,1)S(1)}, u32[]{:S(2)}, u32[]{:S(2)}) collective-permute-start(bf16[32,2,16,32]{3,2,0,1:T(8,128)(2,1)S(1)} %get-tuple-element.26), channel_id=1, source_target_pairs={{16,0},{32,16},{48,32},{64,48},{80,64},{96,80},{112,96},{128,112},... | collective-permute-start | bytes 196616 | tf_op jit(solution)/shard_map/ppermute | solution.py:23
  35.3 7.8 %collective-permute-start.2 = (f32[5,12,2,32]{3,2,1,0:T(2,128)S(1)}, f32[5,12,2,32]{3,2,1,0:T(2,128)S(1)}, u32[]{:S(2)}, u32[]{:S(2)}) collective-permute-start(f32[5,12,2,32]{3,2,1,0:T(2,128)S(1)} %get-tuple-element.48), channel_id=1, source_target_pairs={{0,1},{1,2},{2,3},{3,4},{4,5},{5,6},{6,7},{7,8},{8,9},{9,10},{10,1... | collective-permute-start | bytes 46088 | tf_op jit(solution)/shard_map/ppermute | solution.py:22
  35.4 7.7 %collective-permute-start.3 = (f32[5,12,2,32]{3,2,1,0:T(2,128)S(1)}, f32[5,12,2,32]{3,2,1,0:T(2,128)S(1)}, u32[]{:S(2)}, u32[]{:S(2)}) collective-permute-start(f32[5,12,2,32]{3,2,1,0:T(2,128)S(1)} %get-tuple-element.49), channel_id=1, source_target_pairs={{1,0},{2,1},{3,2},{4,3},{5,4},{6,5},{7,6},{8,7},{9,8},{10,9},{11,1... | collective-permute-start | bytes 46088 | tf_op jit(solution)/shard_map/ppermute | solution.py:23
  45.1 8.5 %collective-permute-start.10 = (bf16[32,12,2,32]{3,2,0,1:T(2,128)(2,1)S(1)}, bf16[32,12,2,32]{3,2,0,1:T(2,128)(2,1)S(1)}, u32[]{:S(2)}, u32[]{:S(2)}) collective-permute-start(bf16[32,12,2,32]{3,2,0,1:T(2,128)(2,1)S(1)} %get-tuple-element.14), channel_id=1, source_target_pairs={{0,1},{1,2},{2,3},{3,4},{4,5},{5,6},{6,7},{7,8},{8,9},{9,10},{10,1... | collective-permute-start | bytes 147464 | tf_op jit(solution)/shard_map/ppermute | solution.py:22
  45.4 8.2 %collective-permute-start.11 = (bf16[32,12,2,32]{3,2,0,1:T(2,128)(2,1)S(1)}, bf16[32,12,2,32]{3,2,0,1:T(2,128)(2,1)S(1)}, u32[]{:S(2)}, u32[]{:S(2)}) collective-permute-start(bf16[32,12,2,32]{3,2,0,1:T(2,128)(2,1)S(1)} %get-tuple-element.15), channel_id=1, source_target_pairs={{1,0},{2,1},{3,2},{4,3},{5,4},{6,5},{7,6},{8,7},{9,8},{10,9},{11,1... | collective-permute-start | bytes 147464 | tf_op jit(solution)/shard_map/ppermute | solution.py:23
  67.5 9.1 %collective-permute-start.12 = (bf16[1,1,16,32]{3,2,1,0:T(8,128)(2,1)S(1)}, bf16[1,1,16,32]{3,2,1,0:T(8,128)(2,1)S(1)}, u32[]{:S(2)}, u32[]{:S(2)}) collective-permute-start(bf16[1,1,16,32]{3,2,1,0:T(8,128)(2,1)S(1)} %get-tuple-element.83), channel_id=1, source_target_pairs={{0,16},{16,32},{32,48},{48,64},{64,80},{80,96},{96,112},{112,128},... | collective-permute-start | bytes 3080 | tf_op jit(solution)/shard_map/ppermute | solution.py:22
  71.5 5.9 %collective-permute-start.13 = (bf16[1,1,16,32]{3,2,1,0:T(8,128)(2,1)S(1)}, bf16[1,1,16,32]{3,2,1,0:T(8,128)(2,1)S(1)}, u32[]{:S(2)}, u32[]{:S(2)}) collective-permute-start(bf16[1,1,16,32]{3,2,1,0:T(8,128)(2,1)S(1)} %get-tuple-element.82), channel_id=1, source_target_pairs={{16,0},{32,16},{48,32},{64,48},{80,64},{96,80},{112,96},{128,112},... | collective-permute-start | bytes 3080 | tf_op jit(solution)/shard_map/ppermute | solution.py:23
  77.5 8.0 %collective-permute-start.14 = (bf16[1,10,1,32]{3,2,1,0:T(2,128)(2,1)S(1)}, bf16[1,10,1,32]{3,2,1,0:T(2,128)(2,1)S(1)}, u32[]{:S(2)}, u32[]{:S(2)}) collective-permute-start(bf16[1,10,1,32]{3,2,1,0:T(2,128)(2,1)S(1)} %get-tuple-element.80), channel_id=1, source_target_pairs={{0,1},{1,2},{2,3},{3,4},{4,5},{5,6},{6,7},{7,8},{8,9},{9,10},{10,1... | collective-permute-start | bytes 1928 | tf_op jit(solution)/shard_map/ppermute | solution.py:22
  77.8 7.8 %collective-permute-start.15 = (bf16[1,10,1,32]{3,2,1,0:T(2,128)(2,1)S(1)}, bf16[1,10,1,32]{3,2,1,0:T(2,128)(2,1)S(1)}, u32[]{:S(2)}, u32[]{:S(2)}) collective-permute-start(bf16[1,10,1,32]{3,2,1,0:T(2,128)(2,1)S(1)} %get-tuple-element.81), channel_id=1, source_target_pairs={{1,0},{2,1},{3,2},{4,3},{5,4},{6,5},{7,6},{8,7},{9,8},{10,9},{11,1... | collective-permute-start | bytes 1928 | tf_op jit(solution)/shard_map/ppermute | solution.py:23
  88.9 5.7 %collective-permute-start.16 = (bf16[32,2,16,32]{3,2,0,1:T(8,128)(2,1)S(1)}, bf16[32,2,16,32]{3,2,0,1:T(8,128)(2,1)S(1)}, u32[]{:S(2)}, u32[]{:S(2)}) collective-permute-start(bf16[32,2,16,32]{3,2,0,1:T(8,128)(2,1)S(1)} %get-tuple-element.25), channel_id=1, source_target_pairs={{0,16},{16,32},{32,48},{48,64},{64,80},{80,96},{96,112},{112,128},... | collective-permute-start | bytes 196616 | tf_op jit(solution)/shard_map/ppermute | solution.py:22
  89.0 6.0 %collective-permute-start.17 = (bf16[32,2,16,32]{3,2,0,1:T(8,128)(2,1)S(1)}, bf16[32,2,16,32]{3,2,0,1:T(8,128)(2,1)S(1)}, u32[]{:S(2)}, u32[]{:S(2)}) collective-permute-start(bf16[32,2,16,32]{3,2,0,1:T(8,128)(2,1)S(1)} %get-tuple-element.24), channel_id=1, source_target_pairs={{16,0},{32,16},{48,32},{64,48},{80,64},{96,80},{112,96},{128,112},... | collective-permute-start | bytes 196616 | tf_op jit(solution)/shard_map/ppermute | solution.py:23
  95.4 8.2 %collective-permute-start.18 = (bf16[32,12,2,32]{3,2,0,1:T(2,128)(2,1)S(1)}, bf16[32,12,2,32]{3,2,0,1:T(2,128)(2,1)S(1)}, u32[]{:S(2)}, u32[]{:S(2)}) collective-permute-start(bf16[32,12,2,32]{3,2,0,1:T(2,128)(2,1)S(1)} %get-tuple-element.12), channel_id=1, source_target_pairs={{0,1},{1,2},{2,3},{3,4},{4,5},{5,6},{6,7},{7,8},{8,9},{9,10},{10,1... | collective-permute-start | bytes 147464 | tf_op jit(solution)/shard_map/ppermute | solution.py:22
  95.5 8.1 %collective-permute-start.19 = (bf16[32,12,2,32]{3,2,0,1:T(2,128)(2,1)S(1)}, bf16[32,12,2,32]{3,2,0,1:T(2,128)(2,1)S(1)}, u32[]{:S(2)}, u32[]{:S(2)}) collective-permute-start(bf16[32,12,2,32]{3,2,0,1:T(2,128)(2,1)S(1)} %get-tuple-element.13), channel_id=1, source_target_pairs={{1,0},{2,1},{3,2},{4,3},{5,4},{6,5},{7,6},{8,7},{9,8},{10,9},{11,1... | collective-permute-start | bytes 147464 | tf_op jit(solution)/shard_map/ppermute | solution.py:23
  116.6 12.4 %copy-start.20 = (bf16[32,8,512]{2,0,1:T(8,128)(2,1)}, bf16[32,8,512]{2,0,1:T(8,128)(2,1)S(1)}, u32[]{:S(2)}) copy-start(bf16[32,8,512]{2,0,1:T(8,128)(2,1)S(1)} %get-tuple-element.28) | copy-start | bytes 786436
  136.7 10.0 %collective-permute-start.20 = (bf16[32,1,16,32]{3,2,0,1:T(8,128)(2,1)S(1)}, bf16[32,1,16,32]{3,2,0,1:T(8,128)(2,1)S(1)}, u32[]{:S(2)}, u32[]{:S(2)}) collective-permute-start(bf16[32,1,16,32]{3,2,0,1:T(8,128)(2,1)S(1)} %get-tuple-element.23), channel_id=1, source_target_pairs={{0,16},{16,32},{32,48},{48,64},{64,80},{80,96},{96,112},{112,128},... | collective-permute-start | bytes 98312 | tf_op jit(solution)/shard_map/ppermute | solution.py:22
  139.0 8.6 %collective-permute-start.21 = (bf16[32,1,16,32]{3,2,0,1:T(8,128)(2,1)S(1)}, bf16[32,1,16,32]{3,2,0,1:T(8,128)(2,1)S(1)}, u32[]{:S(2)}, u32[]{:S(2)}) collective-permute-start(bf16[32,1,16,32]{3,2,0,1:T(8,128)(2,1)S(1)} %get-tuple-element.22), channel_id=1, source_target_pairs={{16,0},{32,16},{48,32},{64,48},{80,64},{96,80},{112,96},{128,112},... | collective-permute-start | bytes 98312 | tf_op jit(solution)/shard_map/ppermute | solution.py:23
  148.0 8.1 %collective-permute-start.22 = (bf16[32,10,1,32]{3,2,0,1:T(2,128)(2,1)S(1)}, bf16[32,10,1,32]{3,2,0,1:T(2,128)(2,1)S(1)}, u32[]{:S(2)}, u32[]{:S(2)}) collective-permute-start(bf16[32,10,1,32]{3,2,0,1:T(2,128)(2,1)S(1)} %get-tuple-element.18), channel_id=1, source_target_pairs={{0,1},{1,2},{2,3},{3,4},{4,5},{5,6},{6,7},{7,8},{8,9},{9,10},{10,1... | collective-permute-start | bytes 61448 | tf_op jit(solution)/shard_map/ppermute | solution.py:22
  148.1 8.0 %collective-permute-start.23 = (bf16[32,10,1,32]{3,2,0,1:T(2,128)(2,1)S(1)}, bf16[32,10,1,32]{3,2,0,1:T(2,128)(2,1)S(1)}, u32[]{:S(2)}, u32[]{:S(2)}) collective-permute-start(bf16[32,10,1,32]{3,2,0,1:T(2,128)(2,1)S(1)} %get-tuple-element.19), channel_id=1, source_target_pairs={{1,0},{2,1},{3,2},{4,3},{5,4},{6,5},{7,6},{8,7},{9,8},{10,9},{11,1... | collective-permute-start | bytes 61448 | tf_op jit(solution)/shard_map/ppermute | solution.py:23
  165.9 13.4 %collective-permute-start.24 = (f32[5,2,16,32]{3,2,1,0:T(8,128)S(1)}, f32[5,2,16,32]{3,2,1,0:T(8,128)S(1)}, u32[]{:S(2)}, u32[]{:S(2)}) collective-permute-start(f32[5,2,16,32]{3,2,1,0:T(8,128)S(1)} %get-tuple-element.50), channel_id=1, source_target_pairs={{0,16},{16,32},{32,48},{48,64},{64,80},{80,96},{96,112},{112,128},... | collective-permute-start | bytes 61448 | tf_op jit(solution)/shard_map/ppermute | solution.py:22
  166.0 13.3 %collective-permute-start.25 = (f32[5,2,16,32]{3,2,1,0:T(8,128)S(1)}, f32[5,2,16,32]{3,2,1,0:T(8,128)S(1)}, u32[]{:S(2)}, u32[]{:S(2)}) collective-permute-start(f32[5,2,16,32]{3,2,1,0:T(8,128)S(1)} %get-tuple-element.51), channel_id=1, source_target_pairs={{16,0},{32,16},{48,32},{64,48},{80,64},{96,80},{112,96},{128,112},... | collective-permute-start | bytes 61448 | tf_op jit(solution)/shard_map/ppermute | solution.py:23
  179.4 7.7 %collective-permute-start.26 = (f32[5,12,2,32]{3,2,1,0:T(2,128)S(1)}, f32[5,12,2,32]{3,2,1,0:T(2,128)S(1)}, u32[]{:S(2)}, u32[]{:S(2)}) collective-permute-start(f32[5,12,2,32]{3,2,1,0:T(2,128)S(1)} %get-tuple-element.46), channel_id=1, source_target_pairs={{0,1},{1,2},{2,3},{3,4},{4,5},{5,6},{6,7},{7,8},{8,9},{9,10},{10,1... | collective-permute-start | bytes 46088 | tf_op jit(solution)/shard_map/ppermute | solution.py:22
  179.9 7.2 %collective-permute-start.27 = (f32[5,12,2,32]{3,2,1,0:T(2,128)S(1)}, f32[5,12,2,32]{3,2,1,0:T(2,128)S(1)}, u32[]{:S(2)}, u32[]{:S(2)}) collective-permute-start(f32[5,12,2,32]{3,2,1,0:T(2,128)S(1)} %get-tuple-element.47), channel_id=1, source_target_pairs={{1,0},{2,1},{3,2},{4,3},{5,4},{6,5},{7,6},{8,7},{9,8},{10,9},{11,1... | collective-permute-start | bytes 46088 | tf_op jit(solution)/shard_map/ppermute | solution.py:23
  210.4 5.6 %collective-permute-start.28 = (bf16[32,1,16,32]{3,2,0,1:T(8,128)(2,1)S(1)}, bf16[32,1,16,32]{3,2,0,1:T(8,128)(2,1)S(1)}, u32[]{:S(2)}, u32[]{:S(2)}) collective-permute-start(bf16[32,1,16,32]{3,2,0,1:T(8,128)(2,1)S(1)} %get-tuple-element.21), channel_id=1, source_target_pairs={{0,16},{16,32},{32,48},{48,64},{64,80},{80,96},{96,112},{112,128},... | collective-permute-start | bytes 98312 | tf_op jit(solution)/shard_map/ppermute | solution.py:22
  211.3 5.7 %collective-permute-start.29 = (bf16[32,1,16,32]{3,2,0,1:T(8,128)(2,1)S(1)}, bf16[32,1,16,32]{3,2,0,1:T(8,128)(2,1)S(1)}, u32[]{:S(2)}, u32[]{:S(2)}) collective-permute-start(bf16[32,1,16,32]{3,2,0,1:T(8,128)(2,1)S(1)} %get-tuple-element.20), channel_id=1, source_target_pairs={{16,0},{32,16},{48,32},{64,48},{80,64},{96,80},{112,96},{128,112},... | collective-permute-start | bytes 98312 | tf_op jit(solution)/shard_map/ppermute | solution.py:23
  217.3 8.3 %collective-permute-start.30 = (bf16[32,10,1,32]{3,2,0,1:T(2,128)(2,1)S(1)}, bf16[32,10,1,32]{3,2,0,1:T(2,128)(2,1)S(1)}, u32[]{:S(2)}, u32[]{:S(2)}) collective-permute-start(bf16[32,10,1,32]{3,2,0,1:T(2,128)(2,1)S(1)} %get-tuple-element.16), channel_id=1, source_target_pairs={{0,1},{1,2},{2,3},{3,4},{4,5},{5,6},{6,7},{7,8},{8,9},{9,10},{10,1... | collective-permute-start | bytes 61448 | tf_op jit(solution)/shard_map/ppermute | solution.py:22
  217.4 8.2 %collective-permute-start.31 = (bf16[32,10,1,32]{3,2,0,1:T(2,128)(2,1)S(1)}, bf16[32,10,1,32]{3,2,0,1:T(2,128)(2,1)S(1)}, u32[]{:S(2)}, u32[]{:S(2)}) collective-permute-start(bf16[32,10,1,32]{3,2,0,1:T(2,128)(2,1)S(1)} %get-tuple-element.17), channel_id=1, source_target_pairs={{1,0},{2,1},{3,2},{4,3},{5,4},{6,5},{7,6},{8,7},{9,8},{10,9},{11,1... | collective-permute-start | bytes 61448 | tf_op jit(solution)/shard_map/ppermute | solution.py:23
  (137 other events, 519.1 us)
Sparse Core Ops, SparseCore 0:
  201.3 251.9 all-reduce.62
where the time goes:
time: 471 us; the launch traced here: 462 us
  waiting for transfers between devices  138 us (29%)
  starting transfers between devices  88.7 us (19%)
  matrix products  85.6 us (18%)
  blocking collectives  85.2 us (18%)
  local copies, waits for them, and re-layouts  25.2 us (5%)
  other arithmetic  22.8 us (5%)
  between operations  17.1 us (4%)
    psum x1, waiting for transfers between devices, shards(): lax.psum((joined[0], joined[1], joined[2], joined[3], joined[4]), ('gx',...  124 us
    psum x1, blocking collectives, shards(): lax.psum((joined[0], joined[1], joined[2], joined[3], joined[4]), ('gx',...  85.2 us
    ppermute x16, starting transfers between devices, extended(): after = lax.ppermute(leading, axis, down)  79.9 us
    dot_general x54, matrix products, conv_middle(): jnp.einsum('cxn,co->oxn', window(hidden, offset[0], offset[1]), conv_mid[...  20.5 us
    dot_general x54, matrix products, retreat(): jnp.einsum('cxn,oxn->co', lift(window(hidden_near, offset[0], offset[1]),...  19.6 us
    dot_general x54, matrix products, conv_middle_back(): jnp.einsum('oxn,co->cxn', window(gradient, -offset[0], -offset[1]), conv_...  17.1 us
    dot_general x54, matrix products, retreat(): jnp.einsum('xn,cxn->c', lift(window(rounded_near, offset[0], offset[1]),...  14.2 us
    dot_general x54, matrix products, conv_first_back(): jnp.einsum('cxn,c->xn', window(gradient, -offset[0], -offset[1]), conv_in...  11.9 us
  transfers between devices with their start and end apart: 33, of which 12 were waited for; matrix products, arithmetic and copies ran while one was open for 12% of the time, Pallas kernels for 0%

commit v1 on v0

v1 whole, which is shorter than its diff:
```python
import math

import jax
import jax.numpy as jnp
import numpy as np
from jax import lax
from jax.experimental import pallas as pl
from jax.experimental.pallas import tpu as pltpu
from jax.sharding import PartitionSpec as P

NZ = 32
C = 32
ROWS = 8
LANES = 512
HALO = 128
WIDE = LANES + 2 * HALO
TALL = 3 * ROWS
time_step = 0.2
MESH = pl.DeviceIdType.MESH
STEPS = (-1, 0, 1)
AROUND = tuple((dx, dy) for dx in STEPS for dy in STEPS if (dx, dy) != (0, 0))
OWN_ROWS = slice(ROWS, 2 * ROWS)
OWN_LANES = slice(HALO, HALO + LANES)
bf16 = jnp.bfloat16
f32 = jnp.float32


def shifted(values, count):
    if count == 0:
        return values
    return pltpu.roll(values, (-count) % values.shape[-1], axis=values.ndim - 1)


def lane_index(values):
    return lax.broadcasted_iota(jnp.int32, values.shape, values.ndim - 1)


def lifted(values, step_z):
    if step_z == 0:
        return values
    edge = NZ - 1 if step_z == 1 else 0
    moved = shifted(values, step_z)
    return jnp.where(lane_index(values) % NZ == edge, jnp.zeros_like(moved), moved)


def own_lanes_only(values):
    lane = lane_index(values)
    return jnp.where((lane >= HALO) & (lane < HALO + LANES), values, jnp.zeros_like(values))


def dot(left, right):
    return lax.dot_general(left, right, (((1,), (0,)), ((), ())), preferred_element_type=f32)


def dot_lanes(left, right):
    return lax.dot_general(left, right, (((1,), (1,)), ((), ())), preferred_element_type=f32)


def central_y(values):
    return 0.5 * (shifted(values, NZ) - shifted(values, -NZ))


def central_z(values):
    return 0.5 * (lifted(values, 1) - lifted(values, -1))


def column_to_row(column):
    size = column.shape[0]
    wide = jnp.broadcast_to(column, (size, size))
    row = lax.broadcasted_iota(jnp.int32, (size, size), 0)
    col = lax.broadcasted_iota(jnp.int32, (size, size), 1)
    return jnp.sum(jnp.where(row == col, wide, 0.0), axis=0, keepdims=True)


def first_stack(field_ext):
    rounded = field_ext[4:20, :].astype(bf16).astype(f32)
    moves = [lifted(shifted(rounded, NZ * b), c) for b in STEPS for c in STEPS]
    return jnp.concatenate(moves, axis=0).astype(bf16)


def z_stack(values, target, sign):
    count = target.shape[0]
    wide = values.astype(f32)
    for number, c in enumerate(STEPS):
        moved = lifted(wide, sign * c).astype(bf16) if c else values
        target[:, number * C : (number + 1) * C, :] = moved.reshape(count, C, WIDE)


def middle_conv(weights, stack, start, sign):
    window = stack[start : start + 5].reshape(5 * 3 * C, WIDE)
    out = dot(weights[...], window).reshape(3, 3, C, WIDE)
    result = out[:, 1]
    for number, b in ((0, -1), (2, 1)):
        part = out[:, number].reshape(3 * C, WIDE)
        result = result + shifted(part, sign * NZ * b).reshape(3, C, WIDE)
    return result


def forward(field_ext, b0, bias_in, w_fwd, bias_mid, stack, hidden_two):
    first = first_stack(field_ext)
    pre = dot(b0[...], first).reshape(14, C, WIDE)
    hidden_one = jnp.tanh(pre + bias_in[...][None]).astype(bf16).reshape(14 * C, WIDE)
    z_stack(hidden_one, stack, 1)
    for start in (0, 3, 6, 9):
        pre = middle_conv(w_fwd, stack, start, 1)
        hidden_two[start : start + 3] = jnp.tanh(pre + bias_mid[...][None]).astype(bf16)
    return first


def stepped(field_ext, kappa, vel, bf, hidden_two):
    flux = dot(bf[...], hidden_two[...].reshape(12 * C, WIDE))
    correction = flux[0:8] + central_y(flux[8:16]) + central_z(flux[16:24])
    here, up, down = field_ext[8:16, :], field_ext[9:17, :], field_ext[7:15, :]
    laplace = (
        up + down + shifted(here, NZ) + shifted(here, -NZ) + lifted(here, 1) + lifted(here, -1)
    )
    laplace = laplace - 6.0 * here
    own = lambda values: values[:, OWN_LANES]
    physics = kappa[...] * own(laplace)
    physics = physics - vel[0] * own(0.5 * (up - down))
    physics = physics - vel[1] * own(central_y(here))
    physics = physics - vel[2] * own(central_z(here))
    return own(here) + time_step * (physics + own(correction))


def cotangent_two(g_ext, bb, hidden_two, grad_two):
    here = g_ext[4:20, :]
    parts = [
        -0.5 * time_step * (g_ext[5:21, :] - g_ext[3:19, :]),
        -time_step * central_y(here),
        -time_step * central_z(here),
    ]
    flux = jnp.concatenate(parts, axis=0)
    high = flux.astype(bf16)
    low = (flux - high.astype(f32)).astype(bf16)
    pair = jnp.concatenate([high, low], axis=0)
    two = hidden_two[...].astype(f32)
    back = dot(bb[...], pair).reshape(12, C, WIDE)
    grad_two[...] = (back * (1.0 - two * two)).astype(bf16)
    return pair


def middle_terms(pair, stack, hidden_two, grad_two, spread):
    own = own_lanes_only(grad_two[2:10].reshape(8 * C, WIDE).astype(f32))
    for number, b in enumerate(STEPS):
        moved = shifted(own, -NZ * b).astype(bf16)
        spread[:, number * C : (number + 1) * C, :] = moved.reshape(8, C, WIDE)
    term_mid = jnp.zeros((9 * C, 3 * C), f32)
    for x in range(ROWS):
        window = stack[x + 2 : x + 5].reshape(9 * C, WIDE)
        term_mid = term_mid + dot_lanes(window, spread[x])
    bias_mid = jnp.sum(jnp.sum(own.reshape(8, C, WIDE), axis=0), axis=1, keepdims=True)
    masked = own_lanes_only(pair.astype(f32)).astype(bf16)
    outer = dot_lanes(hidden_two[2:10].reshape(8 * C, WIDE), masked)
    row_x = lax.broadcasted_iota(jnp.int32, outer.shape, 0) // C
    col = lax.broadcasted_iota(jnp.int32, outer.shape, 1)
    outer = jnp.where(col % 16 == row_x + 4, outer, 0.0)
    outer = jnp.sum(outer.reshape(8, C, outer.shape[1]), axis=0)
    kind = (lax.broadcasted_iota(jnp.int32, outer.shape, 1) // 16) % 3
    term_out = [
        jnp.sum(jnp.where(kind == d, outer, 0.0), axis=1, keepdims=True) for d in range(3)
    ]
    return term_mid, bias_mid, term_out


def cotangent_one(w_bwd, stack, grad_two, grad_stack, grad_one):
    z_stack(grad_two[...].reshape(12 * C, WIDE), grad_stack, -1)
    for start in (0, 3, 6, 7):
        back = middle_conv(w_bwd, grad_stack, start, -1)
        one = stack[start + 2 : start + 5, C : 2 * C, :].astype(f32)
        grad_one[start : start + 3] = (back * (1.0 - one * one)).astype(bf16)


def first_terms(first, grad_one):
    own = own_lanes_only(grad_one[1:9].reshape(8 * C, WIDE).astype(f32))
    outer = dot_lanes(first, own.astype(bf16))
    row_x = lax.broadcasted_iota(jnp.int32, outer.shape, 0) % 16
    col_x = lax.broadcasted_iota(jnp.int32, outer.shape, 1) // C
    parts = []
    for a in range(3):
        kept = jnp.where(row_x - col_x == a + 3, outer, 0.0)
        parts.append(jnp.sum(kept.reshape(9, 16, 8 * C), axis=1))
    folded = jnp.concatenate(parts, axis=0)
    folded = folded[:, :128] + folded[:, 128:]
    folded = folded + pltpu.roll(folded, 64, axis=1)
    folded = folded + pltpu.roll(folded, 32, axis=1)
    bias_in = jnp.sum(jnp.sum(own.reshape(8, C, WIDE), axis=0), axis=1, keepdims=True)
    return folded[:, :C], bias_in


def previous(g_ext, k_ext, v0_ext, v1_ext, vel, bq, grad_one):
    spread = dot(bq[...], grad_one[...].reshape(10 * C, WIDE))
    total = 0.0
    for number, (b, c) in enumerate([(b, c) for b in STEPS for c in STEPS]):
        total = total + lifted(shifted(spread[number * 8 : number * 8 + 8], -NZ * b), -c)
    here = g_ext[8:16, :]
    scaled = k_ext[8:16, :] * here
    up = k_ext[9:17, :] * g_ext[9:17, :]
    down = k_ext[7:15, :] * g_ext[7:15, :]
    physics = up + down + shifted(scaled, NZ) + shifted(scaled, -NZ)
    physics = physics + lifted(scaled, 1) + lifted(scaled, -1) - 6.0 * scaled
    physics = physics + 0.5 * (
        v0_ext[9:17, :] * g_ext[9:17, :] - v0_ext[7:15, :] * g_ext[7:15, :]
    )
    physics = physics + central_y(v1_ext[8:16, :] * here)
    lifted_part = central_z(vel[2] * here[:, OWN_LANES])
    own = lambda values: values[:, OWN_LANES]
    return own(here) + time_step * (own(physics) + lifted_part) + own(total)


def copies_around(ext, send_sem, recv_sem, number, gx, gy, around):
    (me_x, size_x), (me_y, size_y) = gx, gy
    started = []
    for dx, dy in around:
        slot = AROUND.index((dx, dy))
        source = {0: OWN_LANES, 1: slice(LANES, LANES + HALO), -1: slice(HALO, 2 * HALO)}[dy]
        lanes = {0: OWN_LANES, 1: slice(0, HALO), -1: slice(HALO + LANES, WIDE)}[dy]
        rows = {0: OWN_ROWS, 1: slice(0, ROWS), -1: slice(2 * ROWS, TALL)}[dx]
        copy = pltpu.make_async_remote_copy(
            src_ref=ext.at[OWN_ROWS, source],
            dst_ref=ext.at[rows, lanes],
            send_sem=send_sem.at[number, slot],
            recv_sem=recv_sem.at[number, slot],
            device_id=(
                lax.rem(me_x + dx + size_x, size_x),
                lax.rem(me_y + dy + size_y, size_y),
            ),
            device_id_type=MESH,
        )
        copy.start()
        started.append(copy)
    return started


def kernel(
    size_x, size_y, scale,
    field, cotangent, kappa, vel, b0, bias_in, w_fwd, bias_mid, bf, bb, w_bwd, bq,
    out_field, out_in, out_bias_in, out_mid, out_bias_mid, out_out,
    f_ext, f1_ext, g_ext, a_ext, k_ext, v0_ext, v1_ext,
    stack_one, stack_two, two_one, two_two, grad_two, spread, grad_stack, grad_one,
    sums, recv_x, recv_y, gathered,
    send_sem, recv_sem, sum_send, sum_recv,
):
    me_x, me_y = lax.axis_index("gx"), lax.axis_index("gy")
    gx, gy = (me_x, size_x), (me_y, size_y)
    peers = [(lax.rem(me_x + k, size_x), me_y) for k in range(1, size_x)]
    peers += [(me_x, lax.rem(me_y + k, size_y)) for k in range(1, size_y)]
    peers += [
        (lax.rem(me_x + dx + size_x, size_x), lax.rem(me_y + dy + size_y, size_y))
        for dx in (-1, 1)
        for dy in (-1, 1)
    ]
    barrier = pltpu.get_barrier_semaphore()
    for peer in peers:
        pl.semaphore_signal(barrier, inc=1, device_id=peer, device_id_type=MESH)
    for ext, block in (
        (f_ext, field), (g_ext, cotangent), (k_ext, kappa),
        (v0_ext, vel.at[0]), (v1_ext, vel.at[1]),
    ):
        ext[OWN_ROWS, OWN_LANES] = block[...]
    pl.semaphore_wait(barrier, len(peers))

    sides_x, sides_y = ((-1, 0), (1, 0)), ((0, -1), (0, 1))
    send = lambda ext, number, around: copies_around(
        ext, send_sem, recv_sem, number, gx, gy, around
    )
    field_copies = send(f_ext, 0, AROUND)
    g_copies = send(g_ext, 1, AROUND)
    late = send(k_ext, 2, sides_x + sides_y)
    late += send(v0_ext, 3, sides_x) + send(v1_ext, 4, sides_y)

    for copy in field_copies:
        copy.wait_recv()
    first_one = forward(f_ext, b0, bias_in, w_fwd, bias_mid, stack_one, two_one)
    f1_ext[OWN_ROWS, OWN_LANES] = stepped(f_ext, kappa, vel, bf, two_one)
    field_one_copies = send(f1_ext, 5, AROUND)

    for copy in field_one_copies:
        copy.wait_recv()
    first_two = forward(f1_ext, b0, bias_in, w_fwd, bias_mid, stack_two, two_two)

    for copy in g_copies:
        copy.wait_recv()
    pair = cotangent_two(g_ext, bb, two_two, grad_two)
    cotangent_one(w_bwd, stack_two, grad_two, grad_stack, grad_one)
    for copy in late:
        copy.wait_recv()
    a_ext[OWN_ROWS, OWN_LANES] = previous(g_ext, k_ext, v0_ext, v1_ext, vel, bq, grad_one)
    adjoint_copies = send(a_ext, 6, AROUND)
    mid_two, bias_mid_two, out_two = middle_terms(pair, stack_two, two_two, grad_two, spread)
    in_two, bias_in_two = first_terms(first_two, grad_one)

    for copy in adjoint_copies:
        copy.wait_recv()
    pair = cotangent_two(a_ext, bb, two_one, grad_two)
    mid_one, bias_mid_one, out_one = middle_terms(pair, stack_one, two_one, grad_two, spread)
    cotangent_one(w_bwd, stack_one, grad_two, grad_stack, grad_one)
    in_one, bias_in_one = first_terms(first_one, grad_one)

    mid = mid_one + mid_two
    sums[:, 0 : 3 * C] = mid[0 : 8 * C]
    for number in range(3):
        sums[number * C : (number + 1) * C, 3 * C :] = mid[
            8 * C : 9 * C, number * C : (number + 1) * C
        ]
    sums[96:123, 3 * C :] = in_one + in_two
    columns = [bias_in_one + bias_in_two, bias_mid_one + bias_mid_two]
    columns += [one + two for one, two in zip(out_one, out_two)]
    lane = lax.broadcasted_iota(jnp.int32, (C, C), 1)
    block = jnp.zeros((C, C), f32)
    for number, column in enumerate(columns):
        block = jnp.where(lane == number, jnp.broadcast_to(column, (C, C)), block)
    sums[128:160, 3 * C :] = block

    part = sums.shape[0] // size_x
    mine = pl.ds(pl.multiple_of(me_x * part, part), part)
    scatter = []
    for k in range(1, size_x):
        peer = lax.rem(me_x + k, size_x)
        copy = pltpu.make_async_remote_copy(
            src_ref=sums.at[pl.ds(pl.multiple_of(peer * part, part), part)],
            dst_ref=recv_x.at[k],
            send_sem=sum_send.at[0, k],
            recv_sem=sum_recv.at[0, k],
            device_id=(peer, me_y),
            device_id_type=MESH,
        )
        copy.start()
        scatter.append(copy)
    out_field[...] = previous(a_ext, k_ext, v0_ext, v1_ext, vel, bq, grad_one)
    total = sums[mine, :]
    for k, copy in enumerate(scatter):
        copy.wait_recv()
        total = total + recv_x[k + 1]
    recv_y[me_y] = total
    exchange = []
    for k in range(1, size_y):
        copy = pltpu.make_async_remote_copy(
            src_ref=recv_y.at[me_y],
            dst_ref=recv_y.at[me_y],
            send_sem=sum_send.at[1, k],
            recv_sem=sum_recv.at[1, k],
            device_id=(me_x, lax.rem(me_y + k, size_y)),
            device_id_type=MESH,
        )
        copy.start()
        exchange.append(copy)
    for copy in exchange:
        copy.wait_recv()
    total = recv_y[0]
    for k in range(1, size_y):
        total = total + recv_y[k]
    gathered[mine, :] = total * scale
    gather = []
    for k in range(1, size_x):
        copy = pltpu.make_async_remote_copy(
            src_ref=gathered.at[mine],
            dst_ref=gathered.at[mine],
            send_sem=sum_send.at[2, k],
            recv_sem=sum_recv.at[2, k],
            device_id=(lax.rem(me_x + k, size_x), me_y),
            device_id_type=MESH,
        )
        copy.start()
        gather.append(copy)
    for copy in gather:
        copy.wait_recv()

    for a in range(3):
        for b in range(3):
            for c in range(3):
                row = (a * 3 + c) * C
                if row < 8 * C:
                    value = gathered[row : row + C, b * C : (b + 1) * C]
                else:
                    value = gathered[b * C : (b + 1) * C, 3 * C :]
                out_mid[a * 9 + b * 3 + c] = value
    out_in[...] = gathered[96:123, 3 * C :]
    block = gathered[128:160, 3 * C :]
    out_bias_in[...] = column_to_row(block[:, 0:1])
    out_bias_mid[...] = column_to_row(block[:, 1:2])
    out_out[...] = block[:, 2:5]

    everything = field_copies + g_copies + late + field_one_copies + adjoint_copies
    for copy in everything + scatter + exchange + gather:
        copy.wait_send()


def band(rows, cols, place):
    out = np.zeros((3, rows, cols), np.float32)
    for a in range(3):
        for row in range(rows):
            if 0 <= place(row, a) < cols:
                out[a, row, place(row, a)] = 1.0
    return jnp.asarray(out, bf16)


def prepared(conv_in, conv_mid, flux_out):
    first = conv_in.reshape(3, 9, C)
    exact = dict(preferred_element_type=bf16)
    b0 = jnp.einsum("aij,asc->icsj", band(14, 16, lambda i, a: i + a), first, **exact)
    bq = jnp.einsum("axi,asc->sxic", band(8, 10, lambda x, a: x + 2 - a), first, **exact)
    middle = conv_mid.reshape(3, 3, 3, C, C)
    w_fwd = jnp.einsum("axi,abzcd->xbdizc", band(3, 5, lambda x, a: x + a), middle, **exact)
    w_bwd = jnp.einsum("axi,abzcd->xbcizd", band(3, 5, lambda x, a: x + 2 - a), middle, **exact)
    halves = np.zeros((3, 8, 12), np.float32)
    for x in range(8):
        halves[0, x, x + 3], halves[0, x, x + 1] = 0.5, -0.5
        halves[1, x, x + 2] = halves[2, x, x + 2] = 1.0
    bf = jnp.einsum("dxi,cd->dxic", jnp.asarray(halves, bf16), flux_out, **exact)
    pick = np.zeros((2, 12, 16), np.float32)
    for i in range(12):
        pick[:, i, i + 2] = 1.0
    bb = jnp.einsum("hij,cd->ichdj", jnp.asarray(pick, bf16), flux_out, **exact)
    return (
        b0.reshape(14 * C, 144),
        w_fwd.reshape(288, 480),
        bf.reshape(24, 12 * C),
        bb.reshape(12 * C, 96),
        w_bwd.reshape(288, 480),
        bq.reshape(72, 320),
    )


def solution(mesh):
    size_x, size_y = mesh.shape["gx"], mesh.shape["gy"]

    def shards(
        scalar_field, field_cotangent, diffusivity, velocity,
        conv_in, bias_in, conv_mid, bias_mid, flux_out,
    ):
        cells = scalar_field.size * size_x * size_y
        b0, w_fwd, bf, bb, w_bwd, bq = prepared(conv_in, conv_mid, flux_out)
        vmem = pl.BlockSpec(memory_space=pltpu.VMEM)
        ext = pltpu.VMEM((TALL, WIDE), f32)
        part = 256 // size_x
        outs = pl.pallas_call(
            lambda *refs: kernel(size_x, size_y, 1.0 / math.sqrt(cells), *refs),
            out_shape=[
                jax.ShapeDtypeStruct((ROWS, LANES), f32),
                jax.ShapeDtypeStruct((27, C), f32),
                jax.ShapeDtypeStruct((1, C), f32),
                jax.ShapeDtypeStruct((27, C, C), f32),
                jax.ShapeDtypeStruct((1, C), f32),
                jax.ShapeDtypeStruct((C, 3), f32),
            ],
            in_specs=[vmem] * 12,
            out_specs=[vmem] * 6,
            scratch_shapes=[
                ext, ext, ext, ext, ext, ext, ext,
                pltpu.VMEM((14, 3 * C, WIDE), bf16),
                pltpu.VMEM((14, 3 * C, WIDE), bf16),
                pltpu.VMEM((12, C, WIDE), bf16),
                pltpu.VMEM((12, C, WIDE), bf16),
                pltpu.VMEM((12, C, WIDE), bf16),
                pltpu.VMEM((8, 3 * C, WIDE), bf16),
                pltpu.VMEM((12, 3 * C, WIDE), bf16),
                pltpu.VMEM((10, C, WIDE), bf16),
                pltpu.VMEM((256, 128), f32),
                pltpu.VMEM((size_x, part, 128), f32),
                pltpu.VMEM((size_y, part, 128), f32),
                pltpu.VMEM((256, 128), f32),
                pltpu.SemaphoreType.DMA((7, 8)),
                pltpu.SemaphoreType.DMA((7, 8)),
                pltpu.SemaphoreType.DMA((3, max(size_x, size_y))),
                pltpu.SemaphoreType.DMA((3, max(size_x, size_y))),
            ],
            compiler_params=pltpu.CompilerParams(
                collective_id=0, has_side_effects=True, vmem_limit_bytes=48 * 1024 * 1024
            ),
        )(
            scalar_field, field_cotangent, diffusivity, velocity,
            b0, bias_in.reshape(C, 1), w_fwd, bias_mid.reshape(C, 1), bf, bb, w_bwd, bq,
        )
        return (outs[0], outs[1], outs[2].reshape(C), outs[3], outs[4].reshape(C), outs[5])

    return jax.shard_map(
        shards,
        mesh=mesh,
        in_specs=(
            P("gx", "gy"), P("gx", "gy"), P("gx", "gy"), P(None, "gx", "gy"),
            P(), P(), P(), P(), P(),
        ),
        out_specs=(P("gx", "gy"), P(), P(), P(), P(), P()),
        check_vma=False,
    )
```

time: 471 us -> 66.9 us (0.14); the launches traced: 462 us -> 66.8 us
  waiting for transfers between devices: 138 us -> 0 us
  starting transfers between devices: 88.7 us -> 0 us
  blocking collectives: 85.2 us -> 0 us
  matrix products: 85.6 us -> 2.95 us
  Pallas kernels: 0 us -> 52.8 us
  other arithmetic: 22.8 us -> 0.25 us
  between operations: 17.1 us -> 0.95 us
  local copies, waits for them, and re-layouts: 25.2 us -> 9.9 us
    psum x1 -> x0, waiting for transfers between devices: 124 us -> none  [shards(): lax.psum((joined[0], joined[1], joined[2], joined[3], joined[4]), ('gx',...]
    ppermute x32 -> x0, starting transfers between devices: 88.6 us -> none  [the longest x16 79.9 us: extended(): after = lax.ppermute(leading, axis, down)]
    psum x1 -> x0, blocking collectives: 85.2 us -> none  [shards(): lax.psum((joined[0], joined[1], joined[2], joined[3], joined[4]), ('gx',...]
    dot_general x275 -> x4, matrix products: 85.6 us -> 2.95 us  [the longest x1 1.63 us: prepared(): jnp.einsum('axi,abzcd->xbdizc', band(3, 5, lambda x, a: x + a), middle, *...]
    pallas_call x0 -> x1, Pallas kernels: none -> 52.8 us  [shards(): pl.pallas_call(lambda *refs: kernel(size_x, size_y, 1.0 / math.sqrt(cells...]
    ppermute x32 -> x0, waiting for transfers between devices: 14 us -> none  [the longest x16 11.7 us: extended(): before = lax.ppermute(last, axis, up)]
    slice x28 -> x0, local copies, waits for them, and re-layouts: 8.05 us -> none  [the longest x10 5.53 us: window(): values[..., 1 + step_x:row_count - 1 + step_x, (1 + step_y) * NZ:col_coun...]
    concatenate x8 -> x0, other arithmetic: 5.24 us -> none  [extended(): value = jnp.concatenate([before, value, after], axis=dim)]
  transfers between devices with their start and end apart: 33 -> 0, of which waited for: 12 -> 0; matrix products, arithmetic and copies ran while one was open for 12% -> 0% of each run, Pallas kernels for 0% -> 0%
where the time goes in v1:
time: 66.9 us; the launch traced here: 66.8 us
  Pallas kernels  52.8 us (79%)
  local copies, waits for them, and re-layouts  9.9 us (15%)
  matrix products  2.95 us (4%)
  between operations  0.95 us (1%)
    pallas_call x1, Pallas kernels, shards(): pl.pallas_call(lambda *refs: kernel(size_x, size_y, 1.0 / math.sqrt(cells...  52.8 us
    unnamed x34, local copies, waits for them, and re-layouts  3.74 us
    dot_general x1, matrix products, prepared(): jnp.einsum('axi,abzcd->xbdizc', band(3, 5, lambda x, a: x + a), middle, *...  1.63 us
    transpose x1, local copies, waits for them, and re-layouts, prepared(): jnp.einsum('axi,abzcd->xbcizd', band(3, 5, lambda x, a: x + 2 - a), middl...  1.52 us

profile of v1, /device:TPU:1, one launch (start us, length us, event | category | flops | bytes accessed | tf_op | source)
XLA Modules:
  0.0 66.8 jit_solution(2113110886210605792)
XLA Ops:
  0.6 1.6 %convolution_bitcast_fusion.1 = bf16[3,3,32,5,3,32]{2,3,5,4,1,0:T(8,128)(2,1)S(1)} fusion(bf16[3,3,5,1,1,1]{2,0,5,4,3,1:T(4,128)(2,1)} %constant.23, bf16[3,3,3,32,32]{4,3,2,1,0:T(8,128)(2,1)} %bitcast.50), kind=kOutput, calls=%fused_computation.1 | convolution fusion | flops 829440 | bytes 331866 | tf_op jit(solution)/shard_map/axi,abzcd->xbdizc/dot_general | solution.py:404
  2.3 0.0 copy-start.4
  2.3 0.0 copy-start.11
  2.3 1.1 %copy.36 = bf16[3,3,32,5,3,32]{5,4,3,2,1,0:T(4,128)(2,1)S(1)} copy(bf16[3,3,32,5,3,32]{2,3,5,4,1,0:T(8,128)(2,1)S(1)} %convolution_bitcast_fusion.1) | data formatting | bytes 552960 | tf_op jit(solution)/shard_map/axi,abzcd->xbdizc/transpose | solution.py:404
  3.4 0.9 %reshape.52.refs_6_ = bf16[288,480]{1,0:T(8,128)(2,1)S(1)} reshape(bf16[3,3,32,5,3,32]{5,4,3,2,1,0:T(4,128)(2,1)S(1)} %copy.36) | data formatting | bytes 552960 | tf_op jit(solution)/shard_map/reshape | solution.py:417
  4.3 0.0 copy-done.4
  4.3 0.0 copy-done.11
  4.3 0.7 %convolution_bitcast_fusion = bf16[3,3,32,5,3,32]{5,3,2,4,1,0:T(8,128)(2,1)S(1)} fusion(bf16[3,3,5,1,1,1]{2,0,5,4,3,1:T(4,128)(2,1)S(1)} %copy-done.11, bf16[3,3,3,32,32]{4,3,2,1,0:T(8,128)(2,1)S(1)} %bitcast.51), kind=kOutput, calls=%fused_computation | convolution fusion | flops 829440 | bytes 331866 | tf_op jit(solution)/shard_map/axi,abzcd->xbcizd/dot_general | solution.py:405
  5.0 0.0 copy-start.8
  5.0 0.0 copy-start.5
  5.0 1.5 %copy.38 = bf16[3,3,32,5,3,32]{5,4,3,2,1,0:T(4,128)(2,1)S(1)} copy(bf16[3,3,32,5,3,32]{5,3,2,4,1,0:T(8,128)(2,1)S(1)} %convolution_bitcast_fusion) | data formatting | bytes 552960 | tf_op jit(solution)/shard_map/axi,abzcd->xbcizd/transpose | solution.py:405
  6.5 1.0 %reshape.56.refs_10_ = bf16[288,480]{1,0:T(8,128)(2,1)S(1)} reshape(bf16[3,3,32,5,3,32]{5,4,3,2,1,0:T(4,128)(2,1)S(1)} %copy.38) | data formatting | bytes 552960 | tf_op jit(solution)/shard_map/reshape | solution.py:420
  7.6 0.0 copy-done.8
  7.6 0.0 copy-start.7
  7.6 0.0 copy-done.5
  7.6 0.4 convolution_bitcast_fusion.2
  8.0 0.0 copy-start.6
  8.0 0.0 copy-start.10
  8.0 0.2 copy.34
  8.2 0.0 copy-start.9
  8.2 0.0 copy-start.12
  8.2 0.0 copy-start.13
  8.2 0.0 copy-start
  8.2 0.0 copy-start.1
  8.3 0.0 copy-start.2
  8.3 0.0 copy-start.3
  8.3 0.4 reshape.49
  8.7 0.1 copy.41.refs_4_
  8.9 0.0 copy-done.7
  8.9 0.3 convolution_bitcast_fusion.3
  9.2 0.2 reshape.57.refs_11_
  9.4 0.0 copy-done.6
  9.4 0.0 copy-done.10
  9.4 0.1 multiply_bitcast_fusion
  9.5 0.2 reshape.55
  9.8 0.1 copy.44.refs_9_
  9.9 0.0 copy-done.9
  9.9 0.1 broadcast_multiply_fusion
  10.1 0.1 reshape.54.refs_8_
  10.2 0.0 copy-done.12
  10.2 0.1 copy.42.refs_5_
  10.3 0.0 copy-done.13
  10.3 0.1 copy.43.refs_7_
  10.4 0.0 copy-done
  10.4 0.0 copy-done.1
  10.4 0.0 copy-done.2
  10.4 0.0 copy-done.3
  10.4 52.8 %shard_map.193 = (f32[8,512]{1,0:T(8,128)S(1)}, f32[27,32]{1,0:T(8,128)S(1)}, f32[1,32]{1,0:T(1,128)S(1)}, f32[27,32,32]{2,1,0:T(8,128)S(1)}, f32[1,32]{1,0:T(1,128)S(1)}, /*index=5*/f32[32,3]{1,0:T(8,128)S(1)}) custom-call(f32[8,512]{1,0:T(8,128)S(1)} %copy-done.1, f32[8,512]{1,0:T(8,128)S(1)} %copy-done.2, f32[8,512]{1,0:T(8,128)S(1)} %copy-done.3, ...), custom_call_target="tpu_custom_call" | custom-call | tf_op jit(solution)/shard_map/pallas_call | solution.py:437
  63.2 0.7 copy.45
  63.8 0.6 copy.71
  64.4 0.6 copy.72
  65.0 0.5 copy.73
  65.6 0.8 %copy.74 = f32[27,32,32]{2,1,0:T(8,128)} copy(f32[27,32,32]{2,1,0:T(8,128)S(1)} %get-tuple-element.39) | data formatting | bytes 221184
  66.3 0.5 copy.75
  (2 shorter events, 0.0 us)
Async XLA Ops:
  2.3 2.0 %copy-start.4 = (bf16[27,32,32]{2,1,0:T(8,128)(2,1)S(1)}, bf16[27,32,32]{2,1,0:T(8,128)(2,1)}, u32[]{:S(2)}) copy-start(bf16[27,32,32]{2,1,0:T(8,128)(2,1)} %param.21) | copy-start | bytes 165892
  2.3 2.0 %copy-start.11 = (bf16[3,3,5,1,1,1]{2,0,5,4,3,1:T(4,128)(2,1)S(1)}, bf16[3,3,5,1,1,1]{2,0,5,4,3,1:T(4,128)(2,1)}, u32[]{:S(2)}) copy-start(bf16[3,3,5,1,1,1]{2,0,5,4,3,1:T(4,128)(2,1)} %constant.24) | copy-start | bytes 274
  5.0 2.6 %copy-start.8 = (bf16[27,32]{1,0:T(8,128)(2,1)S(1)}, bf16[27,32]{1,0:T(8,128)(2,1)}, u32[]{:S(2)}) copy-start(bf16[27,32]{1,0:T(8,128)(2,1)} %param.19) | copy-start | bytes 5188
  5.0 2.6 %copy-start.5 = (bf16[3,14,16,1]{2,0,3,1:T(4,128)(2,1)S(1)}, bf16[3,14,16,1]{2,0,3,1:T(4,128)(2,1)}, u32[]{:S(2)}) copy-start(bf16[3,14,16,1]{2,0,3,1:T(4,128)(2,1)} %constant.22) | copy-start | bytes 4036
  7.6 1.3 %copy-start.7 = (bf16[3,8,10,1]{2,0,3,1:T(4,128)(2,1)S(1)}, bf16[3,8,10,1]{2,0,3,1:T(4,128)(2,1)}, u32[]{:S(2)}) copy-start(bf16[3,8,10,1]{2,0,3,1:T(4,128)(2,1)} %constant.25) | copy-start | bytes 1444
  8.0 1.4 %copy-start.6 = (bf16[2,12,16]{1,2,0:T(8,128)(2,1)S(1)}, bf16[2,12,16]{1,2,0:T(8,128)(2,1)}, u32[]{:S(2)}) copy-start(bf16[2,12,16]{1,2,0:T(8,128)(2,1)} %constant.17.clone) | copy-start | bytes 2308
  8.0 1.4 %copy-start.10 = (bf16[32,3]{0,1:T(4,128)(2,1)S(1)}, bf16[32,3]{0,1:T(4,128)(2,1)}, u32[]{:S(2)}) copy-start(bf16[32,3]{0,1:T(4,128)(2,1)} %param.23) | copy-start | bytes 580
  8.2 1.7 %copy-start.9 = (bf16[3,8,12]{2,1,0:T(8,128)(2,1)S(1)}, bf16[3,8,12]{2,1,0:T(8,128)(2,1)}, u32[]{:S(2)}) copy-start(bf16[3,8,12]{2,1,0:T(8,128)(2,1)} %constant.16.clone) | copy-start | bytes 1732
  8.2 2.0 %copy-start.12 = (f32[32]{0:T(128)S(1)}, f32[32]{0:T(128)}, u32[]{:S(2)}) copy-start(f32[32]{0:T(128)} %param.20) | copy-start | bytes 388
  8.2 2.1 %copy-start.13 = (f32[32]{0:T(128)S(1)}, f32[32]{0:T(128)}, u32[]{:S(2)}) copy-start(f32[32]{0:T(128)} %param.22) | copy-start | bytes 388
  8.2 2.1 %copy-start = (f32[3,8,512]{2,1,0:T(8,128)S(1)}, f32[3,8,512]{2,1,0:T(8,128)}, u32[]{:S(2)}) copy-start(f32[3,8,512]{2,1,0:T(8,128)} %refs_3_.1) | copy-start | bytes 147460
  8.2 2.1 %copy-start.1 = (f32[8,512]{1,0:T(8,128)S(1)}, f32[8,512]{1,0:T(8,128)}, u32[]{:S(2)}) copy-start(f32[8,512]{1,0:T(8,128)} %refs_0_.1) | copy-start | bytes 49156
  8.3 2.1 %copy-start.2 = (f32[8,512]{1,0:T(8,128)S(1)}, f32[8,512]{1,0:T(8,128)}, u32[]{:S(2)}) copy-start(f32[8,512]{1,0:T(8,128)} %refs_1_.1) | copy-start | bytes 49156
  8.3 2.1 %copy-start.3 = (f32[8,512]{1,0:T(8,128)S(1)}, f32[8,512]{1,0:T(8,128)}, u32[]{:S(2)}) copy-start(f32[8,512]{1,0:T(8,128)} %refs_2_.1) | copy-start | bytes 49156

commit v2 on v1

v2 whole, which is shorter than its diff:
```python
import math

import jax
import jax.numpy as jnp
from jax import lax
from jax.experimental import pallas as pl
from jax.experimental.pallas import tpu as pltpu
from jax.sharding import PartitionSpec as P

NZ = 32
C = 32
ROWS = 8
LANES = 512
HALO = 128
WIDE = LANES + 2 * HALO
TALL = 3 * ROWS
time_step = 0.2
MESH = pl.DeviceIdType.MESH
STEPS = (-1, 0, 1)
AROUND = tuple((dx, dy) for dx in STEPS for dy in STEPS if (dx, dy) != (0, 0))
OWN_ROWS = slice(ROWS, 2 * ROWS)
OWN_LANES = slice(HALO, HALO + LANES)
bf16 = jnp.bfloat16
f32 = jnp.float32


def shifted(values, count):
    if count == 0:
        return values
    return pltpu.roll(values, (-count) % values.shape[-1], axis=values.ndim - 1)


def lane_index(values):
    return lax.broadcasted_iota(jnp.int32, values.shape, values.ndim - 1)


def lifted(values, step_z):
    if step_z == 0:
        return values
    edge = NZ - 1 if step_z == 1 else 0
    moved = shifted(values, step_z)
    return jnp.where(lane_index(values) % NZ == edge, jnp.zeros_like(moved), moved)


def own_lanes_only(values):
    lane = lane_index(values)
    return jnp.where((lane >= HALO) & (lane < HALO + LANES), values, jnp.zeros_like(values))


def dot(left, right):
    return lax.dot_general(left, right, (((1,), (0,)), ((), ())), preferred_element_type=f32)


def dot_lanes(left, right):
    return lax.dot_general(left, right, (((1,), (1,)), ((), ())), preferred_element_type=f32)


def central_y(values):
    return 0.5 * (shifted(values, NZ) - shifted(values, -NZ))


def central_z(values):
    return 0.5 * (lifted(values, 1) - lifted(values, -1))


def column_to_row(column):
    size = column.shape[0]
    wide = jnp.broadcast_to(column, (size, size))
    row = lax.broadcasted_iota(jnp.int32, (size, size), 0)
    col = lax.broadcasted_iota(jnp.int32, (size, size), 1)
    return jnp.sum(jnp.where(row == col, wide, 0.0), axis=0, keepdims=True)


def first_stack(field_ext):
    rounded = field_ext[...].astype(bf16).astype(f32)
    moves = [lifted(shifted(rounded, NZ * b), c) for b in STEPS for c in STEPS]
    stack = jnp.concatenate(moves, axis=0).astype(bf16)
    margin = (stack.shape[1] - WIDE) // 2
    return stack[:, margin : margin + WIDE]


def z_stack(values, target, sign, start):
    count = values.shape[0] // C
    wide = values.astype(f32)
    for number, c in enumerate(STEPS):
        moved = lifted(wide, sign * c).astype(bf16) if c else values
        target[start : start + count, number * C : (number + 1) * C, :] = moved.reshape(
            count, C, WIDE
        )


def middle_conv(weights, stack, start, sign):
    window = stack[start : start + 5].reshape(5 * 3 * C, WIDE)
    out = dot(weights[...], window).reshape(3, 3, C, WIDE)
    result = out[:, 1]
    for number, b in ((0, -1), (2, 1)):
        part = out[:, number].reshape(3 * C, WIDE)
        result = result + shifted(part, sign * NZ * b).reshape(3, C, WIDE)
    return result


def forward(field_ext, near, weights, stack, hidden_two):
    b0, bias_in, w_fwd, bias_mid = weights
    first = first_stack(field_ext)
    low, high = (1, 15) if near else (0, 16)
    pre = dot(b0[low * C : high * C, :], first).reshape(high - low, C, WIDE)
    hidden_one = jnp.tanh(pre + bias_in[...][None]).astype(bf16)
    z_stack(hidden_one.reshape((high - low) * C, WIDE), stack, 1, low)
    for start in (1, 4, 7, 10) if near else (0, 3, 6, 9, 11):
        pre = middle_conv(w_fwd, stack, start, 1)
        hidden_two[start : start + 3] = jnp.tanh(pre + bias_mid[...][None]).astype(bf16)
    return first


def stepped(field_ext, kv_ext, bf, hidden_two):
    flux = dot(bf[...], hidden_two[1:13].reshape(12 * C, WIDE))
    correction = flux[0:8] + central_y(flux[8:16]) + central_z(flux[16:24])
    here, up, down = field_ext[8:16, :], field_ext[9:17, :], field_ext[7:15, :]
    laplace = (
        up + down + shifted(here, NZ) + shifted(here, -NZ) + lifted(here, 1) + lifted(here, -1)
    )
    laplace = laplace - 6.0 * here
    own = lambda values: values[:, OWN_LANES]
    cell = lambda number: kv_ext[number, OWN_ROWS, OWN_LANES]
    physics = cell(0) * own(laplace)
    physics = physics - cell(1) * own(0.5 * (up - down))
    physics = physics - cell(2) * own(central_y(here))
    physics = physics - cell(3) * own(central_z(here))
    return own(here) + time_step * (physics + own(correction))


def row_moved(values, count):
    return pltpu.roll(values, (-count) % values.shape[0], axis=0)


def flux_pair(here):
    parts = [
        -0.5 * time_step * (row_moved(here, 1) - row_moved(here, -1)),
        -time_step * central_y(here),
        -time_step * central_z(here),
    ]
    flux = jnp.concatenate(parts, axis=0)
    high = flux.astype(bf16)
    low = (flux - high.astype(f32)).astype(bf16)
    return jnp.concatenate([high, low], axis=0)


def cotangent_two(back, hidden_two, low, high):
    two = hidden_two[low:high].astype(f32)
    return (back.reshape(high - low, C, WIDE) * (1.0 - two * two)).astype(bf16)


def middle_terms(stack, own_two, spread):
    own = own_lanes_only(own_two.astype(f32))
    for number, b in enumerate(STEPS):
        moved = shifted(own, -NZ * b).astype(bf16)
        spread[:, number * C : (number + 1) * C, :] = moved.reshape(8, C, WIDE)
    term_mid = jnp.zeros((9 * C, 3 * C), f32)
    for x in range(ROWS):
        window = stack[x + 3 : x + 6].reshape(9 * C, WIDE)
        term_mid = term_mid + dot_lanes(window, spread[x])
    return term_mid


def out_terms(pair, hidden_two, own_two):
    own = own_lanes_only(own_two.astype(f32))
    bias_mid = jnp.sum(jnp.sum(own.reshape(8, C, WIDE), axis=0), axis=1, keepdims=True)
    masked = own_lanes_only(pair.astype(f32)).astype(bf16)
    outer = dot_lanes(hidden_two[3:11].reshape(8 * C, WIDE), masked)
    row_x = lax.broadcasted_iota(jnp.int32, outer.shape, 0) // C
    col = lax.broadcasted_iota(jnp.int32, outer.shape, 1)
    outer = jnp.where(col % 16 == row_x + 4, outer, 0.0)
    outer = jnp.sum(outer.reshape(8, C, outer.shape[1]), axis=0)
    kind = (lax.broadcasted_iota(jnp.int32, outer.shape, 1) // 16) % 3
    columns = [jnp.sum(jnp.where(kind == d, outer, 0.0), axis=1, keepdims=True) for d in range(3)]
    return [column_to_row(column) for column in [bias_mid] + columns]


def cotangent_one(w_bwd, stack, grad_stack, grad_one, starts):
    for start in starts:
        back = middle_conv(w_bwd, grad_stack, start, -1)
        one = stack[start + 2 : start + 5, C : 2 * C, :].astype(f32)
        grad_one[start : start + 3] = (back * (1.0 - one * one)).astype(bf16)


def first_terms(first, grad_one):
    own = own_lanes_only(grad_one[2:10].reshape(8 * C, WIDE).astype(f32))
    outer = dot_lanes(first, own.astype(bf16))
    row_x = lax.broadcasted_iota(jnp.int32, outer.shape, 0) % TALL
    col_x = lax.broadcasted_iota(jnp.int32, outer.shape, 1) // C
    parts = []
    for a in range(3):
        kept = jnp.where(row_x - col_x == a + 7, outer, 0.0)
        parts.append(jnp.sum(kept.reshape(9, TALL, 8 * C), axis=1))
    folded = jnp.concatenate(parts, axis=0)
    folded = folded[:, :128] + folded[:, 128:]
    folded = folded + pltpu.roll(folded, 64, axis=1)
    folded = folded + pltpu.roll(folded, 32, axis=1)
    bias_in = jnp.sum(jnp.sum(own.reshape(8, C, WIDE), axis=0), axis=1, keepdims=True)
    return folded[:, :C], column_to_row(bias_in)


def previous(here, kv_ext, bq, grad_one):
    spread = dot(bq[...], grad_one[...].reshape(12 * C, WIDE))
    total = 0.0
    for number, (b, c) in enumerate([(b, c) for b in STEPS for c in STEPS]):
        total = total + lifted(shifted(spread[number * 16 : number * 16 + 16], -NZ * b), -c)
    cell = lambda number: kv_ext[number, 4:20, :]
    scaled = cell(0) * here
    physics = row_moved(scaled, 1) + row_moved(scaled, -1) - 6.0 * scaled
    physics = physics + shifted(scaled, NZ) + shifted(scaled, -NZ)
    physics = physics + lifted(scaled, 1) + lifted(scaled, -1)
    scaled = cell(1) * here
    physics = physics + 0.5 * (row_moved(scaled, 1) - row_moved(scaled, -1))
    physics = physics + central_y(cell(2) * here) + central_z(cell(3) * here)
    return here + time_step * physics + total


def iota(shape, dimension):
    return lax.broadcasted_iota(jnp.int32, shape, dimension)


def ones_where(condition):
    return jnp.where(condition, 1.0, 0.0).astype(bf16)


def dot_rows(left, right):
    return lax.dot_general(left, right, (((0,), (0,)), ((), ())), preferred_element_type=f32)


def place_middle(conv_mid, wide, w_fwd, w_bwd):
    for target, backward in ((w_fwd, False), (w_bwd, True)):
        wide[...] = jnp.zeros_like(wide)
        for a in range(3):
            for b in range(3):
                for c in range(3):
                    block = conv_mid[a * 9 + b * 3 + c].astype(f32)
                    if not backward:
                        block = block.T
                    for x in range(3):
                        row = (x * 3 + b) * C
                        col = ((x + (2 - a if backward else a)) * 3 + c) * C
                        wide[row : row + C, col : col + C] = block
        target[...] = wide[...].astype(bf16)


def place_first(conv_in, b0, bq):
    taps = conv_in[...]
    shape = (27, 9 * TALL)
    spread = []
    for a in range(3):
        pick = ones_where(iota(shape, 0) == iota(shape, 1) // TALL + 9 * a)
        spread.append(dot_rows(taps, pick))
    j = iota(spread[0].shape, 1) % TALL
    for i in range(16):
        rows = sum(jnp.where(j == 3 + i + a, spread[a], 0.0) for a in range(3))
        b0[i * C : (i + 1) * C, :] = rows.astype(bf16)
    shape = (C, 12 * C)
    tiled = dot(taps, ones_where(iota(shape, 1) % C == iota(shape, 0))).astype(bf16)
    total = 0.0
    for a in range(3):
        pick = ones_where(iota((144, 27), 1) == iota((144, 27), 0) // 16 + 9 * a)
        rows = dot(pick, tiled)
        kept = iota(rows.shape, 1) // C == iota(rows.shape, 0) % 16 - a - 1
        total = total + jnp.where(kept, rows, 0.0)
    bq[...] = total.astype(bf16)


def place_flux(flux, bf, bb):
    taps = flux[...]
    shape = (C, 12 * C)
    tiled = dot(taps, ones_where(iota(shape, 1) % C == iota(shape, 0))).astype(bf16)
    rows = dot(ones_where(iota((24, 3), 1) == iota((24, 3), 0) // 8), tiled)
    x, i = iota(rows.shape, 0) % 8, iota(rows.shape, 1) // C
    first = iota(rows.shape, 0) < 8
    factor = jnp.where(i == x + 3, 0.5, jnp.where(i == x + 1, -0.5, 0.0))
    factor = jnp.where(first, factor, jnp.where(i == x + 2, 1.0, 0.0))
    bf[...] = (rows * factor).astype(bf16)
    pick = ones_where(iota((3, 96), 0) == (iota((3, 96), 1) // 16) % 3)
    columns = dot_rows(taps, pick)
    j = iota(columns.shape, 1) % 16
    for i in range(14):
        bb[i * C : (i + 1) * C, :] = jnp.where(j == i + 1, columns, 0.0).astype(bf16)


def row_to_column(row):
    size = row.shape[1]
    wide = jnp.broadcast_to(row, (size, size))
    return jnp.sum(
        jnp.where(iota((size, size), 0) == iota((size, size), 1), wide, 0.0),
        axis=1,
        keepdims=True,
    )


def remote(source, target, sems, peer):
    copy = pltpu.make_async_remote_copy(
        src_ref=source,
        dst_ref=target,
        send_sem=sems[0],
        recv_sem=sems[1],
        device_id=peer,
        device_id_type=MESH,
    )
    copy.start()


def send_around(ext, sems, place):
    (me_x, size_x), (me_y, size_y) = place
    width = ext.shape[-1]
    side = (width - LANES) // 2
    lead = (slice(None),) * (len(ext.shape) - 2)
    sources = {0: slice(side, side + LANES), 1: slice(LANES, side + LANES), -1: slice(side, 2 * side)}
    targets = {0: slice(side, side + LANES), 1: slice(0, side), -1: slice(side + LANES, width)}
    rows = {0: OWN_ROWS, 1: slice(0, ROWS), -1: slice(2 * ROWS, TALL)}
    for dx, dy in AROUND:
        peer = (
            lax.rem(me_x + dx + size_x, size_x),
            lax.rem(me_y + dy + size_y, size_y),
        )
        source = ext.at[lead + (OWN_ROWS, sources[dy])]
        remote(source, ext.at[lead + (rows[dx], targets[dy])], sems, peer)
    depth = ext.shape[0] if lead else 1
    return depth * (3 * width - LANES) // 128


def wait_tiles(sem, gauge, count):
    part = gauge.at[pl.ds(0, 8 * count)]
    pltpu.make_async_copy(part, part, sem).wait()


def kernel(
    size_x, size_y, scale,
    field, cotangent, kappa, vel, conv_in_in, bias_in_in, conv_mid_in, bias_mid_in, flux_in,
    out_field, out_sums, out_small,
    f_ext, f1_ext, g_ext, a_ext, kv_ext, conv_in, bias_in_row, conv_mid, bias_mid_row, flux,
    bias_in, bias_mid, wide, b0, w_fwd, bf, bb, w_bwd, bq,
    stack_one, stack_two, two_one, two_two, back_two, spread, grad_stack, grad_one,
    sums, recv_x, recv_y, gathered, small, small_x, small_y, gauge,
    local_sem, send_sem, recv_sem,
):
    me_x, me_y = lax.axis_index("gx"), lax.axis_index("gy")
    place = (me_x, size_x), (me_y, size_y)
    half_x, half_y = size_x // 2, size_y // 2
    mine_hi = lax.div(me_y, half_y)
    peers_x = [(lax.rem(me_x + k, size_x), me_y) for k in range(1, size_x)]
    peers_y = []
    for k in range(1, size_y):
        other = lax.rem(me_y + k, size_y)
        flip = lax.rem(mine_hi + lax.div(other, half_y), 2) * half_x
        peers_y.append((lax.rem(me_x + flip, size_x), other))
    near = [
        (lax.rem(me_x + dx + size_x, size_x), lax.rem(me_y + dy + size_y, size_y))
        for dx, dy in AROUND
        if dy != 0
    ]
    barrier = pltpu.get_barrier_semaphore()
    for peer in near + peers_x + peers_y:
        pl.semaphore_signal(barrier, inc=1, device_id=peer, device_id_type=MESH)
    own = (OWN_ROWS, OWN_LANES)
    arrivals = []
    for source, target in (
        (field, f_ext.at[own]),
        (cotangent, g_ext.at[own]),
        (kappa, kv_ext.at[(0,) + own]),
        (vel, kv_ext.at[(slice(1, 4),) + own]),
        (conv_in_in, conv_in),
        (bias_in_in, bias_in_row),
        (conv_mid_in, conv_mid),
        (bias_mid_in, bias_mid_row),
        (flux_in, flux),
    ):
        copy = pltpu.make_async_copy(source, target, local_sem.at[len(arrivals)])
        copy.start()
        arrivals.append(copy)
    for copy in arrivals:
        copy.wait()
    sems = lambda number: (send_sem.at[number], recv_sem.at[number])
    pl.semaphore_wait(barrier, len(near + peers_x + peers_y))
    tiles = [send_around(f_ext, sems(0), place), send_around(g_ext, sems(1), place)]
    tiles.append(send_around(kv_ext, sems(2), place))

    bias_in[...] = row_to_column(bias_in_row[...])
    bias_mid[...] = row_to_column(bias_mid_row[...])
    place_first(conv_in, b0, bq)
    place_middle(conv_mid, wide, w_fwd, w_bwd)
    place_flux(flux, bf, bb)

    weights = (b0, bias_in, w_fwd, bias_mid)
    wait_tiles(recv_sem.at[0], gauge, tiles[0])
    first_one = forward(f_ext, True, weights, stack_one, two_one)
    f1_ext[OWN_ROWS, 256 : 256 + LANES] = stepped(f_ext, kv_ext, bf, two_one)
    tiles.append(send_around(f1_ext, sems(3), place))

    wait_tiles(recv_sem.at[1], gauge, tiles[1])
    pair_two = flux_pair(g_ext[4:20, :])
    back_two[...] = dot(bb[...], pair_two)
    wait_tiles(recv_sem.at[3], gauge, tiles[3])
    first_two = forward(f1_ext, False, weights, stack_two, two_two)

    grad_two = cotangent_two(back_two[...], two_two, 0, 14).reshape(14 * C, WIDE)
    z_stack(grad_two, grad_stack, -1, 0)
    cotangent_one(w_bwd, stack_two, grad_stack, grad_one, (0, 3, 6, 9))
    wait_tiles(recv_sem.at[2], gauge, tiles[2])
    adjoint = previous(g_ext[4:20, :], kv_ext, bq, grad_one)
    a_ext[own] = adjoint[4:12, OWN_LANES]
    tiles.append(send_around(a_ext, sems(4), place))

    own_two = grad_two[3 * C : 11 * C]
    mid = middle_terms(stack_two, own_two, spread)
    pair_one = flux_pair(adjoint)
    own_one = cotangent_two(dot(bb[3 * C : 11 * C, :], pair_one), two_one, 3, 11)
    own_one = own_one.reshape(8 * C, WIDE)
    mid = mid + middle_terms(stack_one, own_one, spread)
    sums[:, 0 : 3 * C] = mid[0 : 8 * C]
    for number in range(3):
        sums[number * C : (number + 1) * C, 3 * C :] = mid[
            8 * C : 9 * C, number * C : (number + 1) * C
        ]
    sums[3 * C :, 3 * C :] = jnp.zeros((5 * C, C), f32)

    part = sums.shape[0] // size_x
    share = lambda x: pl.ds(
        pl.multiple_of(lax.rem(x + mine_hi * half_x, size_x) * part, part), part
    )
    for peer in peers_x:
        remote(sums.at[share(peer[0])], recv_x.at[me_x], sems(5), peer)

    in_two, bias_in_two = first_terms(first_two, grad_one)
    rows_two = out_terms(pair_two, two_two, own_two)
    rows_one = out_terms(pair_one, two_one, own_one)
    wait_tiles(recv_sem.at[4], gauge, tiles[4])
    here = a_ext[4:20, :]
    full = cotangent_two(dot(bb[C : 13 * C, :], flux_pair(here)), two_one, 1, 13)
    z_stack(full.reshape(12 * C, WIDE), grad_stack, -1, 1)
    cotangent_one(w_bwd, stack_one, grad_stack, grad_one, (1, 4, 7, 8))
    in_one, bias_in_one = first_terms(first_one, grad_one)
    matrix = jnp.concatenate(
        [in_one + in_two, bias_in_one + bias_in_two]
        + [one + two for one, two in zip(rows_one, rows_two)],
        axis=0,
    )
    for number in range(4):
        small[:, number * C : (number + 1) * C] = matrix[number * 8 : number * 8 + 8]
    small_x[me_x] = small[...]

    per = part // 8
    wait_tiles(recv_sem.at[5], gauge, per * (size_x - 1))
    recv_x[me_x] = sums[share(me_x), :]
    total = recv_x[0]
    for k in range(1, size_x):
        total = total + recv_x[k]
    recv_y[me_y] = total
    for peer in peers_y:
        remote(recv_y.at[me_y], recv_y.at[me_y], sems(6), peer)
    for peer in peers_x:
        remote(small, small_x.at[me_x], sems(8), peer)

    final = previous(here, kv_ext, bq, grad_one)
    out_field[...] = final[4:12, OWN_LANES]

    wait_tiles(recv_sem.at[8], gauge, size_x - 1)
    total = small_x[0]
    for k in range(1, size_x):
        total = total + small_x[k]
    small_y[me_y] = total
    for peer in peers_y:
        remote(small_y.at[me_y], small_y.at[me_y], sems(9), peer)

    wait_tiles(recv_sem.at[6], gauge, per * (size_y - 1))
    total = recv_y[0]
    for k in range(1, size_y):
        total = total + recv_y[k]
    gathered[share(me_x), :] = total * scale
    for peer in peers_x:
        remote(gathered.at[share(me_x)], gathered.at[share(me_x)], sems(7), peer)

    wait_tiles(recv_sem.at[9], gauge, size_y - 1)
    total = small_y[0]
    for k in range(1, size_y):
        total = total + small_y[k]
    out_small[...] = total * scale
    wait_tiles(recv_sem.at[7], gauge, per * (size_x - 1))
    out_sums[...] = gathered[...]

    for number in range(5):
        wait_tiles(send_sem.at[number], gauge, tiles[number])
    wait_tiles(send_sem.at[5], gauge, per * (size_x - 1))
    wait_tiles(send_sem.at[6], gauge, per * (size_y - 1))
    wait_tiles(send_sem.at[7], gauge, per * (size_x - 1))
    wait_tiles(send_sem.at[8], gauge, size_x - 1)
    wait_tiles(send_sem.at[9], gauge, size_y - 1)


def unpack(field, sums, small, out_field, out_in, out_bias_in, out_mid, out_bias_mid, out_out):
    out_field[...] = field[...]
    for a in range(3):
        for b in range(3):
            for c in range(3):
                row = (a * 3 + c) * C
                if row < 8 * C:
                    value = sums[row : row + C, b * C : (b + 1) * C]
                else:
                    value = sums[b * C : (b + 1) * C, 3 * C :]
                out_mid[a * 9 + b * 3 + c] = value
    for number in range(3):
        out_in[number * 8 : number * 8 + 8] = small[:, number * C : (number + 1) * C]
    last = small[:, 3 * C :]
    out_in[24:27] = last[0:3]
    out_bias_in[...] = last[3:4]
    out_bias_mid[...] = last[4:5]
    out_out[...] = last[5:8]


def solution(mesh):
    size_x, size_y = mesh.shape["gx"], mesh.shape["gy"]

    def shards(
        scalar_field, field_cotangent, diffusivity, velocity,
        conv_in, bias_in, conv_mid, bias_mid, flux_out,
    ):
        cells = scalar_field.size * size_x * size_y
        vmem = pl.BlockSpec(memory_space=pltpu.VMEM)
        anywhere = pl.BlockSpec(memory_space=pltpu.HBM)
        part = 256 // size_x
        ext = pltpu.VMEM((TALL, WIDE), f32)
        shape = jax.ShapeDtypeStruct
        outs = pl.pallas_call(
            lambda *refs: kernel(size_x, size_y, 1.0 / math.sqrt(cells), *refs),
            out_shape=[shape((ROWS, LANES), f32), shape((256, 128), f32), shape((8, 128), f32)],
            in_specs=[anywhere] * 9,
            out_specs=[vmem] * 3,
            scratch_shapes=[
                ext, pltpu.VMEM((TALL, WIDE + 256), f32), ext, ext,
                pltpu.VMEM((4, TALL, WIDE), f32),
                pltpu.VMEM((27, C), bf16),
                pltpu.VMEM((1, C), f32),
                pltpu.VMEM((27, C, C), bf16),
                pltpu.VMEM((1, C), f32),
                pltpu.VMEM((3, C), bf16),
                pltpu.VMEM((C, 1), f32),
                pltpu.VMEM((C, 1), f32),
                pltpu.VMEM((288, 480), f32),
                pltpu.VMEM((16 * C, 9 * TALL), bf16),
                pltpu.VMEM((288, 480), bf16),
                pltpu.VMEM((24, 12 * C), bf16),
                pltpu.VMEM((14 * C, 96), bf16),
                pltpu.VMEM((288, 480), bf16),
                pltpu.VMEM((144, 12 * C), bf16),
                pltpu.VMEM((16, 3 * C, WIDE), bf16),
                pltpu.VMEM((16, 3 * C, WIDE), bf16),
                pltpu.VMEM((14, C, WIDE), bf16),
                pltpu.VMEM((14, C, WIDE), bf16),
                pltpu.VMEM((14 * C, WIDE), f32),
                pltpu.VMEM((8, 3 * C, WIDE), bf16),
                pltpu.VMEM((14, 3 * C, WIDE), bf16),
                pltpu.VMEM((12, C, WIDE), bf16),
                pltpu.VMEM((256, 128), f32),
                pltpu.VMEM((size_x, part, 128), f32),
                pltpu.VMEM((size_y, part, 128), f32),
                pltpu.VMEM((256, 128), f32),
                pltpu.VMEM((8, 128), f32),
                pltpu.VMEM((size_x, 8, 128), f32),
                pltpu.VMEM((size_y, 8, 128), f32),
                pltpu.VMEM((448, 128), f32),
                pltpu.SemaphoreType.DMA((9,)),
                pltpu.SemaphoreType.DMA((10,)),
                pltpu.SemaphoreType.DMA((10,)),
            ],
            compiler_params=pltpu.CompilerParams(
                collective_id=0, has_side_effects=True, vmem_limit_bytes=60 * 1024 * 1024
            ),
        )(
            scalar_field, field_cotangent, diffusivity, velocity,
            conv_in, bias_in.reshape(1, C), conv_mid, bias_mid.reshape(1, C), flux_out.T,
        )
        outs = pl.pallas_call(
            unpack,
            out_shape=[
                shape((ROWS, LANES), f32),
                shape((27, C), f32),
                shape((1, C), f32),
                shape((27, C, C), f32),
                shape((1, C), f32),
                shape((3, C), f32),
            ],
            in_specs=[vmem] * 3,
            out_specs=[vmem] * 6,
        )(*outs)
        return (outs[0], outs[1], outs[2].reshape(C), outs[3], outs[4].reshape(C), outs[5].T)

    return jax.shard_map(
        shards,
        mesh=mesh,
        in_specs=(
            P("gx", "gy"), P("gx", "gy"), P("gx", "gy"), P(None, "gx", "gy"),
            P(), P(), P(), P(), P(),
        ),
        out_specs=(P("gx", "gy"), P(), P(), P(), P(), P()),
        check_vma=False,
    )
```

time: 66.9 us -> 47.6 us (0.71)
  local copies, waits for them, and re-layouts: 9.9 us -> 0 us
  Pallas kernels: 52.8 us -> 46.8 us
  matrix products: 2.95 us -> 0 us
    pallas_call x1, Pallas kernels: 52.8 us -> 44.9 us  [shards(): pl.pallas_call(lambda *refs: kernel(size_x, size_y, 1.0 / math.sqrt(cells...]
    unnamed x34 -> x0, local copies, waits for them, and re-layouts: 3.74 us -> none
    reshape x11 -> x0, local copies, waits for them, and re-layouts: 3.33 us -> none  [the longest x1 1.03 us: prepared(): w_bwd.reshape(288, 480)]
    dot_general x4 -> x0, matrix products: 2.95 us -> none  [the longest x1 1.63 us: prepared(): jnp.einsum('axi,abzcd->xbdizc', band(3, 5, lambda x, a: x + a), middle, *...]
    transpose x4 -> x0, local copies, waits for them, and re-layouts: 2.83 us -> none  [the longest x1 1.52 us: prepared(): jnp.einsum('axi,abzcd->xbcizd', band(3, 5, lambda x, a: x + 2 - a), middl...]
    pallas_call x0 -> x1, Pallas kernels: none -> 1.82 us  [shards(): pl.pallas_call(unpack, out_shape=[shape((ROWS, LANES), f32), shape((27, C...]
where the time goes in v2:
time: 47.6 us; the launch traced here: 47.4 us
  Pallas kernels  46.8 us (98%)
  between operations  0.64 us (1%)
    pallas_call x1, Pallas kernels, shards(): pl.pallas_call(lambda *refs: kernel(size_x, size_y, 1.0 / math.sqrt(cells...  44.9 us
    pallas_call x1, Pallas kernels, shards(): pl.pallas_call(unpack, out_shape=[shape((ROWS, LANES), f32), shape((27, C...  1.82 us

profile of v2, /device:TPU:1, one launch (start us, length us, event | category | flops | bytes accessed | tf_op | source)
XLA Modules:
  0.0 47.4 jit_solution(5797169208782990170)
XLA Ops:
  0.6 44.9 %shard_map.136 = (f32[8,512]{1,0:T(8,128)}, f32[256,128]{1,0:T(8,128)}, f32[8,128]{1,0:T(8,128)}) custom-call(f32[8,512]{1,0:T(8,128)} %refs_0_.1, f32[8,512]{1,0:T(8,128)} %refs_1_.1, f32[8,512]{1,0:T(8,128)} %refs_2_.1, f32[3,8,512]{2,1,0:T(8,128)} %refs_3_.1, bf16[27,32]{1,0:T(8,128)(2,1)} %refs_4_.1, f32[1,32]{1,0:T(1,128)} %bitcast.7, ...), custom_call_target="tpu_custom_call" | custom-call | tf_op jit(solution)/shard_map/pallas_call | solution.py:528
  45.6 1.8 %shard_map.137 = (f32[8,512]{1,0:T(8,128)}, f32[27,32]{1,0:T(8,128)}, f32[1,32]{1,0:T(1,128)}, f32[27,32,32]{2,1,0:T(8,128)}, f32[1,32]{1,0:T(1,128)}, /*index=5*/f32[3,32]{1,0:T(4,128)}) custom-call(f32[8,512]{1,0:T(8,128)} %get-tuple-element.15.field, f32[256,128]{1,0:T(8,128)} %get-tuple-element.16.sums, f32[8,128]{1,0:T(8,128)} %get-tuple-element.17.small), custom_call_target="tpu_custom_call" | custom-call | tf_op jit(solution)/shard_map/pallas_call | solution.py:577

commit v3 on v2

--- a/solution.py
+++ b/solution.py
@@ -14,10 +14,12 @@
 HALO = 128
 WIDE = LANES + 2 * HALO
 TALL = 3 * ROWS
+BROAD = WIDE + 256
+MIDDLE = slice(128, 128 + WIDE)
 time_step = 0.2
 MESH = pl.DeviceIdType.MESH
 STEPS = (-1, 0, 1)
-AROUND = tuple((dx, dy) for dx in STEPS for dy in STEPS if (dx, dy) != (0, 0))
+AROUND = ((1, 1), (1, -1), (-1, 1), (-1, -1), (0, 1), (0, -1), (1, 0), (-1, 0))
 OWN_ROWS = slice(ROWS, 2 * ROWS)
 OWN_LANES = slice(HALO, HALO + LANES)
 bf16 = jnp.bfloat16
@@ -74,59 +76,54 @@
 def first_stack(field_ext):
     rounded = field_ext[...].astype(bf16).astype(f32)
     moves = [lifted(shifted(rounded, NZ * b), c) for b in STEPS for c in STEPS]
-    stack = jnp.concatenate(moves, axis=0).astype(bf16)
-    margin = (stack.shape[1] - WIDE) // 2
-    return stack[:, margin : margin + WIDE]
+    return jnp.concatenate(moves, axis=0).astype(bf16)
 
 
 def z_stack(values, target, sign, start):
-    count = values.shape[0] // C
+    count, width = values.shape[0] // C, values.shape[1]
     wide = values.astype(f32)
     for number, c in enumerate(STEPS):
         moved = lifted(wide, sign * c).astype(bf16) if c else values
         target[start : start + count, number * C : (number + 1) * C, :] = moved.reshape(
-            count, C, WIDE
+            count, C, width
         )
 
 
 def middle_conv(weights, stack, start, sign):
-    window = stack[start : start + 5].reshape(5 * 3 * C, WIDE)
-    out = dot(weights[...], window).reshape(3, 3, C, WIDE)
+    width = stack.shape[2]
+    window = stack[start : start + 5].reshape(5 * 3 * C, width)
+    out = dot(weights[...], window).reshape(3, 3, C, width)
     result = out[:, 1]
     for number, b in ((0, -1), (2, 1)):
-        part = out[:, number].reshape(3 * C, WIDE)
-        result = result + shifted(part, sign * NZ * b).reshape(3, C, WIDE)
+        part = out[:, number].reshape(3 * C, width)
+        result = result + shifted(part, sign * NZ * b).reshape(3, C, width)
     return result
 
 
-def forward(field_ext, near, weights, stack, hidden_two):
+def forward(first, low, weights, stack, hidden_two):
     b0, bias_in, w_fwd, bias_mid = weights
-    first = first_stack(field_ext)
-    low, high = (1, 15) if near else (0, 16)
-    pre = dot(b0[low * C : high * C, :], first).reshape(high - low, C, WIDE)
+    count, width = stack.shape[0], stack.shape[2]
+    pre = dot(b0[low * C : (low + count) * C, :], first).reshape(count, C, width)
     hidden_one = jnp.tanh(pre + bias_in[...][None]).astype(bf16)
-    z_stack(hidden_one.reshape((high - low) * C, WIDE), stack, 1, low)
-    for start in (1, 4, 7, 10) if near else (0, 3, 6, 9, 11):
+    z_stack(hidden_one.reshape(count * C, width), stack, 1, 0)
+    for start in [*range(0, count - 5, 3), count - 5]:
         pre = middle_conv(w_fwd, stack, start, 1)
         hidden_two[start : start + 3] = jnp.tanh(pre + bias_mid[...][None]).astype(bf16)
-    return first
 
 
 def stepped(field_ext, kv_ext, bf, hidden_two):
-    flux = dot(bf[...], hidden_two[1:13].reshape(12 * C, WIDE))
-    correction = flux[0:8] + central_y(flux[8:16]) + central_z(flux[16:24])
-    here, up, down = field_ext[8:16, :], field_ext[9:17, :], field_ext[7:15, :]
+    flux = dot(bf[...], hidden_two[...].reshape(20 * C, BROAD))
+    correction = flux[0:TALL] + central_y(flux[TALL : 2 * TALL]) + central_z(flux[2 * TALL :])
+    here = field_ext[...]
+    up, down = row_moved(here, 1), row_moved(here, -1)
     laplace = (
         up + down + shifted(here, NZ) + shifted(here, -NZ) + lifted(here, 1) + lifted(here, -1)
     )
-    laplace = laplace - 6.0 * here
-    own = lambda values: values[:, OWN_LANES]
-    cell = lambda number: kv_ext[number, OWN_ROWS, OWN_LANES]
-    physics = cell(0) * own(laplace)
-    physics = physics - cell(1) * own(0.5 * (up - down))
-    physics = physics - cell(2) * own(central_y(here))
-    physics = physics - cell(3) * own(central_z(here))
-    return own(here) + time_step * (physics + own(correction))
+    physics = kv_ext[0] * (laplace - 6.0 * here)
+    physics = physics - kv_ext[1] * (0.5 * (up - down))
+    physics = physics - kv_ext[2] * central_y(here)
+    physics = physics - kv_ext[3] * central_z(here)
+    return here + time_step * (physics + correction)
 
 
 def row_moved(values, count):
@@ -146,19 +143,26 @@
 
 
 def cotangent_two(back, hidden_two, low, high):
-    two = hidden_two[low:high].astype(f32)
+    two = centre(hidden_two, low, high).astype(f32)
     return (back.reshape(high - low, C, WIDE) * (1.0 - two * two)).astype(bf16)
 
 
+def centre(ref, low, high):
+    margin = (ref.shape[2] - WIDE) // 2
+    return ref[low:high, :, margin : margin + WIDE]
+
+
 def middle_terms(stack, own_two, spread):
+    first_row = (stack.shape[0] - ROWS) // 2 - 1
     own = own_lanes_only(own_two.astype(f32))
     for number, b in enumerate(STEPS):
         moved = shifted(own, -NZ * b).astype(bf16)
         spread[:, number * C : (number + 1) * C, :] = moved.reshape(8, C, WIDE)
-    term_mid = jnp.zeros((9 * C, 3 * C), f32)
-    for x in range(ROWS):
-        window = stack[x + 3 : x + 6].reshape(9 * C, WIDE)
-        term_mid = term_mid + dot_lanes(window, spread[x])
+    pairs = jnp.zeros((12 * C, 6 * C), f32)
+    for x in range(0, ROWS, 2):
+        window = centre(stack, first_row + x, first_row + x + 4).reshape(12 * C, WIDE)
+        pairs = pairs + dot_lanes(window, spread[x : x + 2].reshape(6 * C, WIDE))
+    term_mid = pairs[0 : 9 * C, 0 : 3 * C] + pairs[3 * C :, 3 * C :]
     return term_mid
 
 
@@ -166,7 +170,9 @@
     own = own_lanes_only(own_two.astype(f32))
     bias_mid = jnp.sum(jnp.sum(own.reshape(8, C, WIDE), axis=0), axis=1, keepdims=True)
     masked = own_lanes_only(pair.astype(f32)).astype(bf16)
-    outer = dot_lanes(hidden_two[3:11].reshape(8 * C, WIDE), masked)
+    first_row = (hidden_two.shape[0] - ROWS) // 2
+    two = centre(hidden_two, first_row, first_row + ROWS)
+    outer = dot_lanes(two.reshape(8 * C, WIDE), masked)
     row_x = lax.broadcasted_iota(jnp.int32, outer.shape, 0) // C
     col = lax.broadcasted_iota(jnp.int32, outer.shape, 1)
     outer = jnp.where(col % 16 == row_x + 4, outer, 0.0)
@@ -179,7 +185,8 @@
 def cotangent_one(w_bwd, stack, grad_stack, grad_one, starts):
     for start in starts:
         back = middle_conv(w_bwd, grad_stack, start, -1)
-        one = stack[start + 2 : start + 5, C : 2 * C, :].astype(f32)
+        low = start + (stack.shape[0] - 12) // 2
+        one = centre(stack, low, low + 3)[:, C : 2 * C].astype(f32)
         grad_one[start : start + 3] = (back * (1.0 - one * one)).astype(bf16)
 
 
@@ -205,7 +212,7 @@
     total = 0.0
     for number, (b, c) in enumerate([(b, c) for b in STEPS for c in STEPS]):
         total = total + lifted(shifted(spread[number * 16 : number * 16 + 16], -NZ * b), -c)
-    cell = lambda number: kv_ext[number, 4:20, :]
+    cell = lambda number: kv_ext[number, 4:20, MIDDLE]
     scaled = cell(0) * here
     physics = row_moved(scaled, 1) + row_moved(scaled, -1) - 6.0 * scaled
     physics = physics + shifted(scaled, NZ) + shifted(scaled, -NZ)
@@ -252,8 +259,8 @@
         pick = ones_where(iota(shape, 0) == iota(shape, 1) // TALL + 9 * a)
         spread.append(dot_rows(taps, pick))
     j = iota(spread[0].shape, 1) % TALL
-    for i in range(16):
-        rows = sum(jnp.where(j == 3 + i + a, spread[a], 0.0) for a in range(3))
+    for i in range(22):
+        rows = sum(jnp.where(j == i + a, spread[a], 0.0) for a in range(3))
         b0[i * C : (i + 1) * C, :] = rows.astype(bf16)
     shape = (C, 12 * C)
     tiled = dot(taps, ones_where(iota(shape, 1) % C == iota(shape, 0))).astype(bf16)
@@ -268,13 +275,14 @@
 
 def place_flux(flux, bf, bb):
     taps = flux[...]
-    shape = (C, 12 * C)
+    shape = (C, 20 * C)
     tiled = dot(taps, ones_where(iota(shape, 1) % C == iota(shape, 0))).astype(bf16)
-    rows = dot(ones_where(iota((24, 3), 1) == iota((24, 3), 0) // 8), tiled)
-    x, i = iota(rows.shape, 0) % 8, iota(rows.shape, 1) // C
-    first = iota(rows.shape, 0) < 8
-    factor = jnp.where(i == x + 3, 0.5, jnp.where(i == x + 1, -0.5, 0.0))
-    factor = jnp.where(first, factor, jnp.where(i == x + 2, 1.0, 0.0))
+    shape = (3 * TALL, 3)
+    rows = dot(ones_where(iota(shape, 1) == iota(shape, 0) // TALL), tiled)
+    x, i = iota(rows.shape, 0) % TALL, iota(rows.shape, 1) // C
+    first = iota(rows.shape, 0) < TALL
+    factor = jnp.where(i == x - 1, 0.5, jnp.where(i == x - 3, -0.5, 0.0))
+    factor = jnp.where(first, factor, jnp.where(i == x - 2, 1.0, 0.0))
     bf[...] = (rows * factor).astype(bf16)
     pick = ones_where(iota((3, 96), 0) == (iota((3, 96), 1) // 16) % 3)
     columns = dot_rows(taps, pick)
@@ -329,13 +337,41 @@
     pltpu.make_async_copy(part, part, sem).wait()
 
 
+def far_first_x(me_x, me_y, size):
+    groups, ring, cores = (2, size // 4, 2) if size % 8 == 0 else (1, size, 1)
+    steps = [
+        (g, r, c) for g in range(groups) for r in range(ring) for c in range(cores)
+    ][1:]
+    steps.sort(key=lambda step: (-step[0] - min(step[1], ring - step[1]), -step[2]))
+    at = lax.div(me_x, ring * cores), lax.rem(lax.div(me_x, cores), ring), lax.rem(me_x, cores)
+    peers = []
+    for g, r, c in steps:
+        to = lax.rem(at[0] + g, groups), lax.rem(at[1] + r, ring), lax.rem(at[2] + c, cores)
+        peers.append(((to[0] * ring + to[1]) * cores + to[2], me_y))
+    return peers
+
+
+def far_first_y(me_x, me_y, size_x, size_y):
+    ring = size_y // 2
+    steps = [(g, r) for g in range(2) for r in range(ring)][1:]
+    steps.sort(key=lambda step: -step[0] - min(step[1], ring - step[1]))
+    high, at = lax.div(me_y, ring), lax.rem(me_y, ring)
+    return [
+        (
+            lax.rem(me_x + g * (size_x // 2), size_x),
+            lax.rem(high + g, 2) * ring + lax.rem(at + r, ring),
+        )
+        for g, r in steps
+    ]
+
+
 def kernel(
     size_x, size_y, scale,
     field, cotangent, kappa, vel, conv_in_in, bias_in_in, conv_mid_in, bias_mid_in, flux_in,
     out_field, out_sums, out_small,
     f_ext, f1_ext, g_ext, a_ext, kv_ext, conv_in, bias_in_row, conv_mid, bias_mid_row, flux,
     bias_in, bias_mid, wide, b0, w_fwd, bf, bb, w_bwd, bq,
-    stack_one, stack_two, two_one, two_two, back_two, spread, grad_stack, grad_one,
+    stack_one, stack_two, two_one, two_two, spread, grad_stack, grad_one,
     sums, recv_x, recv_y, gathered, small, small_x, small_y, gauge,
     local_sem, send_sem, recv_sem,
 ):
@@ -343,27 +379,23 @@
     place = (me_x, size_x), (me_y, size_y)
     half_x, half_y = size_x // 2, size_y // 2
     mine_hi = lax.div(me_y, half_y)
-    peers_x = [(lax.rem(me_x + k, size_x), me_y) for k in range(1, size_x)]
-    peers_y = []
-    for k in range(1, size_y):
-        other = lax.rem(me_y + k, size_y)
-        flip = lax.rem(mine_hi + lax.div(other, half_y), 2) * half_x
-        peers_y.append((lax.rem(me_x + flip, size_x), other))
+    peers_x, peers_y = far_first_x(me_x, me_y, size_x), far_first_y(me_x, me_y, size_x, size_y)
     near = [
         (lax.rem(me_x + dx + size_x, size_x), lax.rem(me_y + dy + size_y, size_y))
         for dx, dy in AROUND
         if dy != 0
     ]
     barrier = pltpu.get_barrier_semaphore()
-    for peer in near + peers_x + peers_y:
+    for peer in peers_y + near + peers_x:
         pl.semaphore_signal(barrier, inc=1, device_id=peer, device_id_type=MESH)
     own = (OWN_ROWS, OWN_LANES)
+    broad_own = (OWN_ROWS, slice(256, 256 + LANES))
     arrivals = []
     for source, target in (
-        (field, f_ext.at[own]),
+        (field, f_ext.at[broad_own]),
         (cotangent, g_ext.at[own]),
-        (kappa, kv_ext.at[(0,) + own]),
-        (vel, kv_ext.at[(slice(1, 4),) + own]),
+        (kappa, kv_ext.at[(0,) + broad_own]),
+        (vel, kv_ext.at[(slice(1, 4),) + broad_own]),
         (conv_in_in, conv_in),
         (bias_in_in, bias_in_row),
         (conv_mid_in, conv_mid),
@@ -377,8 +409,9 @@
         copy.wait()
     sems = lambda number: (send_sem.at[number], recv_sem.at[number])
     pl.semaphore_wait(barrier, len(near + peers_x + peers_y))
-    tiles = [send_around(f_ext, sems(0), place), send_around(g_ext, sems(1), place)]
-    tiles.append(send_around(kv_ext, sems(2), place))
+    tiles = [
+        send_around(ext, sems(number), place) for number, ext in enumerate((f_ext, kv_ext, g_ext))
+    ]
 
     bias_in[...] = row_to_column(bias_in_row[...])
     bias_mid[...] = row_to_column(bias_mid_row[...])
@@ -388,28 +421,28 @@
 
     weights = (b0, bias_in, w_fwd, bias_mid)
     wait_tiles(recv_sem.at[0], gauge, tiles[0])
-    first_one = forward(f_ext, True, weights, stack_one, two_one)
-    f1_ext[OWN_ROWS, 256 : 256 + LANES] = stepped(f_ext, kv_ext, bf, two_one)
-    tiles.append(send_around(f1_ext, sems(3), place))
-
+    first_one = first_stack(f_ext)
+    forward(first_one, 0, weights, stack_one, two_one)
+    first_one = first_one[:, MIDDLE]
     wait_tiles(recv_sem.at[1], gauge, tiles[1])
+    f1_ext[...] = stepped(f_ext, kv_ext, bf, two_one)
+    first_two = first_stack(f1_ext)[:, MIDDLE]
+    forward(first_two, 3, weights, stack_two, two_two)
+
+    wait_tiles(recv_sem.at[2], gauge, tiles[2])
     pair_two = flux_pair(g_ext[4:20, :])
-    back_two[...] = dot(bb[...], pair_two)
-    wait_tiles(recv_sem.at[3], gauge, tiles[3])
-    first_two = forward(f1_ext, False, weights, stack_two, two_two)
-
-    grad_two = cotangent_two(back_two[...], two_two, 0, 14).reshape(14 * C, WIDE)
+    back_two = dot(bb[...], pair_two)
+    grad_two = cotangent_two(back_two, two_two, 0, 14).reshape(14 * C, WIDE)
     z_stack(grad_two, grad_stack, -1, 0)
     cotangent_one(w_bwd, stack_two, grad_stack, grad_one, (0, 3, 6, 9))
-    wait_tiles(recv_sem.at[2], gauge, tiles[2])
     adjoint = previous(g_ext[4:20, :], kv_ext, bq, grad_one)
     a_ext[own] = adjoint[4:12, OWN_LANES]
-    tiles.append(send_around(a_ext, sems(4), place))
+    tiles.append(send_around(a_ext, sems(3), place))
 
     own_two = grad_two[3 * C : 11 * C]
     mid = middle_terms(stack_two, own_two, spread)
     pair_one = flux_pair(adjoint)
-    own_one = cotangent_two(dot(bb[3 * C : 11 * C, :], pair_one), two_one, 3, 11)
+    own_one = cotangent_two(dot(bb[3 * C : 11 * C, :], pair_one), two_one, 6, 14)
     own_one = own_one.reshape(8 * C, WIDE)
     mid = mid + middle_terms(stack_one, own_one, spread)
     sums[:, 0 : 3 * C] = mid[0 : 8 * C]
@@ -424,14 +457,14 @@
         pl.multiple_of(lax.rem(x + mine_hi * half_x, size_x) * part, part), part
     )
     for peer in peers_x:
-        remote(sums.at[share(peer[0])], recv_x.at[me_x], sems(5), peer)
+        remote(sums.at[share(peer[0])], recv_x.at[me_x], sems(4), peer)
 
     in_two, bias_in_two = first_terms(first_two, grad_one)
     rows_two = out_terms(pair_two, two_two, own_two)
     rows_one = out_terms(pair_one, two_one, own_one)
-    wait_tiles(recv_sem.at[4], gauge, tiles[4])
+    wait_tiles(recv_sem.at[3], gauge, tiles[3])
     here = a_ext[4:20, :]
-    full = cotangent_two(dot(bb[C : 13 * C, :], flux_pair(here)), two_one, 1, 13)
+    full = cotangent_two(dot(bb[C : 13 * C, :], flux_pair(here)), two_one, 4, 16)
     z_stack(full.reshape(12 * C, WIDE), grad_stack, -1, 1)
     cotangent_one(w_bwd, stack_one, grad_stack, grad_one, (1, 4, 7, 8))
     in_one, bias_in_one = first_terms(first_one, grad_one)
@@ -445,51 +478,51 @@
     small_x[me_x] = small[...]
 
     per = part // 8
-    wait_tiles(recv_sem.at[5], gauge, per * (size_x - 1))
+    wait_tiles(recv_sem.at[4], gauge, per * (size_x - 1))
     recv_x[me_x] = sums[share(me_x), :]
     total = recv_x[0]
     for k in range(1, size_x):
         total = total + recv_x[k]
     recv_y[me_y] = total
     for peer in peers_y:
-        remote(recv_y.at[me_y], recv_y.at[me_y], sems(6), peer)
+        remote(recv_y.at[me_y], recv_y.at[me_y], sems(5), peer)
     for peer in peers_x:
-        remote(small, small_x.at[me_x], sems(8), peer)
+        remote(small, small_x.at[me_x], sems(7), peer)
 
     final = previous(here, kv_ext, bq, grad_one)
     out_field[...] = final[4:12, OWN_LANES]
 
-    wait_tiles(recv_sem.at[8], gauge, size_x - 1)
+    wait_tiles(recv_sem.at[7], gauge, size_x - 1)
     total = small_x[0]
     for k in range(1, size_x):
         total = total + small_x[k]
     small_y[me_y] = total
     for peer in peers_y:
-        remote(small_y.at[me_y], small_y.at[me_y], sems(9), peer)
-
-    wait_tiles(recv_sem.at[6], gauge, per * (size_y - 1))
+        remote(small_y.at[me_y], small_y.at[me_y], sems(8), peer)
+
+    wait_tiles(recv_sem.at[5], gauge, per * (size_y - 1))
     total = recv_y[0]
     for k in range(1, size_y):
         total = total + recv_y[k]
     gathered[share(me_x), :] = total * scale
     for peer in peers_x:
-        remote(gathered.at[share(me_x)], gathered.at[share(me_x)], sems(7), peer)
-
-    wait_tiles(recv_sem.at[9], gauge, size_y - 1)
+        remote(gathered.at[share(me_x)], gathered.at[share(me_x)], sems(6), peer)
+
+    wait_tiles(recv_sem.at[8], gauge, size_y - 1)
     total = small_y[0]
     for k in range(1, size_y):
         total = total + small_y[k]
     out_small[...] = total * scale
-    wait_tiles(recv_sem.at[7], gauge, per * (size_x - 1))
+    wait_tiles(recv_sem.at[6], gauge, per * (size_x - 1))
     out_sums[...] = gathered[...]
 
-    for number in range(5):
+    for number in range(4):
         wait_tiles(send_sem.at[number], gauge, tiles[number])
-    wait_tiles(send_sem.at[5], gauge, per * (size_x - 1))
-    wait_tiles(send_sem.at[6], gauge, per * (size_y - 1))
-    wait_tiles(send_sem.at[7], gauge, per * (size_x - 1))
-    wait_tiles(send_sem.at[8], gauge, size_x - 1)
-    wait_tiles(send_sem.at[9], gauge, size_y - 1)
+    wait_tiles(send_sem.at[4], gauge, per * (size_x - 1))
+    wait_tiles(send_sem.at[5], gauge, per * (size_y - 1))
+    wait_tiles(send_sem.at[6], gauge, per * (size_x - 1))
+    wait_tiles(send_sem.at[7], gauge, size_x - 1)
+    wait_tiles(send_sem.at[8], gauge, size_y - 1)
 
 
 def unpack(field, sums, small, out_field, out_in, out_bias_in, out_mid, out_bias_mid, out_out):
@@ -523,7 +556,7 @@
         vmem = pl.BlockSpec(memory_space=pltpu.VMEM)
         anywhere = pl.BlockSpec(memory_space=pltpu.HBM)
         part = 256 // size_x
-        ext = pltpu.VMEM((TALL, WIDE), f32)
+        ext, broad = pltpu.VMEM((TALL, WIDE), f32), pltpu.VMEM((TALL, BROAD), f32)
         shape = jax.ShapeDtypeStruct
         outs = pl.pallas_call(
             lambda *refs: kernel(size_x, size_y, 1.0 / math.sqrt(cells), *refs),
@@ -531,8 +564,8 @@
             in_specs=[anywhere] * 9,
             out_specs=[vmem] * 3,
             scratch_shapes=[
-                ext, pltpu.VMEM((TALL, WIDE + 256), f32), ext, ext,
-                pltpu.VMEM((4, TALL, WIDE), f32),
+                broad, broad, ext, ext,
+                pltpu.VMEM((4, TALL, BROAD), f32),
                 pltpu.VMEM((27, C), bf16),
                 pltpu.VMEM((1, C), f32),
                 pltpu.VMEM((27, C, C), bf16),
@@ -541,17 +574,16 @@
                 pltpu.VMEM((C, 1), f32),
                 pltpu.VMEM((C, 1), f32),
                 pltpu.VMEM((288, 480), f32),
-                pltpu.VMEM((16 * C, 9 * TALL), bf16),
+                pltpu.VMEM((22 * C, 9 * TALL), bf16),
                 pltpu.VMEM((288, 480), bf16),
-                pltpu.VMEM((24, 12 * C), bf16),
+                pltpu.VMEM((3 * TALL, 20 * C), bf16),
                 pltpu.VMEM((14 * C, 96), bf16),
                 pltpu.VMEM((288, 480), bf16),
                 pltpu.VMEM((144, 12 * C), bf16),
+                pltpu.VMEM((22, 3 * C, BROAD), bf16),
                 pltpu.VMEM((16, 3 * C, WIDE), bf16),
-                pltpu.VMEM((16, 3 * C, WIDE), bf16),
+                pltpu.VMEM((20, C, BROAD), bf16),
                 pltpu.VMEM((14, C, WIDE), bf16),
-                pltpu.VMEM((14, C, WIDE), bf16),
-                pltpu.VMEM((14 * C, WIDE), f32),
                 pltpu.VMEM((8, 3 * C, WIDE), bf16),
                 pltpu.VMEM((14, 3 * C, WIDE), bf16),
                 pltpu.VMEM((12, C, WIDE), bf16),
@@ -562,10 +594,10 @@
                 pltpu.VMEM((8, 128), f32),
                 pltpu.VMEM((size_x, 8, 128), f32),
                 pltpu.VMEM((size_y, 8, 128), f32),
-                pltpu.VMEM((448, 128), f32),
+                pltpu.VMEM((640, 128), f32),
                 pltpu.SemaphoreType.DMA((9,)),
-                pltpu.SemaphoreType.DMA((10,)),
-                pltpu.SemaphoreType.DMA((10,)),
+                pltpu.SemaphoreType.DMA((9,)),
+                pltpu.SemaphoreType.DMA((9,)),
             ],
             compiler_params=pltpu.CompilerParams(
                 collective_id=0, has_side_effects=True, vmem_limit_bytes=60 * 1024 * 1024

time: 47.6 us -> 45.6 us (0.958)
  Pallas kernels: 46.8 us -> 44.8 us
    pallas_call x1, Pallas kernels: 44.9 us -> 42.9 us  [shards(): pl.pallas_call(lambda *refs: kernel(size_x, size_y, 1.0 / math.sqrt(cells...]
where the time goes in v3:
time: 45.6 us; the launch traced here: 45.4 us
  Pallas kernels  44.8 us (98%)
  between operations  0.64 us (1%)
    pallas_call x1, Pallas kernels, shards(): pl.pallas_call(lambda *refs: kernel(size_x, size_y, 1.0 / math.sqrt(cells...  42.9 us
    pallas_call x1, Pallas kernels, shards(): pl.pallas_call(unpack, out_shape=[shape((ROWS, LANES), f32), shape((27, C...  1.82 us

profile of v3, /device:TPU:1, one launch (start us, length us, event | category | flops | bytes accessed | tf_op | source)
XLA Modules:
  0.0 45.4 jit_solution(597168463616363461)
XLA Ops:
  0.6 42.9 %shard_map.136 = (f32[8,512]{1,0:T(8,128)}, f32[256,128]{1,0:T(8,128)}, f32[8,128]{1,0:T(8,128)}) custom-call(f32[8,512]{1,0:T(8,128)} %refs_0_.1, f32[8,512]{1,0:T(8,128)} %refs_1_.1, f32[8,512]{1,0:T(8,128)} %refs_2_.1, f32[3,8,512]{2,1,0:T(8,128)} %refs_3_.1, bf16[27,32]{1,0:T(8,128)(2,1)} %refs_4_.1, f32[1,32]{1,0:T(1,128)} %bitcast.7, ...), custom_call_target="tpu_custom_call" | custom-call | tf_op jit(solution)/shard_map/pallas_call | solution.py:561
  43.6 1.8 %shard_map.137 = (f32[8,512]{1,0:T(8,128)}, f32[27,32]{1,0:T(8,128)}, f32[1,32]{1,0:T(1,128)}, f32[27,32,32]{2,1,0:T(8,128)}, f32[1,32]{1,0:T(1,128)}, /*index=5*/f32[3,32]{1,0:T(4,128)}) custom-call(f32[8,512]{1,0:T(8,128)} %get-tuple-element.15.field, f32[256,128]{1,0:T(8,128)} %get-tuple-element.16.sums, f32[8,128]{1,0:T(8,128)} %get-tuple-element.17.small), custom_call_target="tpu_custom_call" | custom-call | tf_op jit(solution)/shard_map/pallas_call | solution.py:609

commit v4 on v3

--- a/solution.py
+++ b/solution.py
@@ -75,7 +75,8 @@
 
 def first_stack(field_ext):
     rounded = field_ext[...].astype(bf16).astype(f32)
-    moves = [lifted(shifted(rounded, NZ * b), c) for b in STEPS for c in STEPS]
+    rows = [shifted(rounded, NZ * b) for b in STEPS]
+    moves = [lifted(row, c) for row in rows for c in STEPS]
     return jnp.concatenate(moves, axis=0).astype(bf16)
 
 
@@ -89,26 +90,35 @@
         )
 
 
-def middle_conv(weights, stack, start, sign):
+def middle_conv(weights, stack, start, count, sign):
     width = stack.shape[2]
-    window = stack[start : start + 5].reshape(5 * 3 * C, width)
-    out = dot(weights[...], window).reshape(3, 3, C, width)
+    window = stack[start : start + count + 2].reshape((count + 2) * 3 * C, width)
+    banded = weights[0 : count * 3 * C, 0 : (count + 2) * 3 * C]
+    out = dot(banded, window).reshape(count, 3, C, width)
     result = out[:, 1]
     for number, b in ((0, -1), (2, 1)):
-        part = out[:, number].reshape(3 * C, width)
-        result = result + shifted(part, sign * NZ * b).reshape(3, C, width)
+        part = out[:, number].reshape(count * C, width)
+        result = result + shifted(part, sign * NZ * b).reshape(count, C, width)
     return result
+
+
+def groups(low, high):
+    return [(start, min(3, high - start)) for start in range(low, high, 3)]
 
 
 def forward(first, low, weights, stack, hidden_two):
     b0, bias_in, w_fwd, bias_mid = weights
     count, width = stack.shape[0], stack.shape[2]
     pre = dot(b0[low * C : (low + count) * C, :], first).reshape(count, C, width)
-    hidden_one = jnp.tanh(pre + bias_in[...][None]).astype(bf16)
-    z_stack(hidden_one.reshape(count * C, width), stack, 1, 0)
-    for start in [*range(0, count - 5, 3), count - 5]:
-        pre = middle_conv(w_fwd, stack, start, 1)
-        hidden_two[start : start + 3] = jnp.tanh(pre + bias_mid[...][None]).astype(bf16)
+    filled = 0
+    for start, rows in groups(0, count - 2):
+        until = min(start + rows + 5, count) if start else 5
+        if start == 0 or until > filled:
+            hidden_one = jnp.tanh(pre[filled:until] + bias_in[...][None]).astype(bf16)
+            z_stack(hidden_one.reshape((until - filled) * C, width), stack, 1, filled)
+            filled = until
+        out = middle_conv(w_fwd, stack, start, rows, 1)
+        hidden_two[start : start + rows] = jnp.tanh(out + bias_mid[...][None]).astype(bf16)
 
 
 def stepped(field_ext, kv_ext, bf, hidden_two):
@@ -182,12 +192,12 @@
     return [column_to_row(column) for column in [bias_mid] + columns]
 
 
-def cotangent_one(w_bwd, stack, grad_stack, grad_one, starts):
-    for start in starts:
-        back = middle_conv(w_bwd, grad_stack, start, -1)
-        low = start + (stack.shape[0] - 12) // 2
-        one = centre(stack, low, low + 3)[:, C : 2 * C].astype(f32)
-        grad_one[start : start + 3] = (back * (1.0 - one * one)).astype(bf16)
+def cotangent_one(w_bwd, stack, grad_stack, grad_one, low, high):
+    for start, rows in groups(low, high):
+        back = middle_conv(w_bwd, grad_stack, start, rows, -1)
+        first = start + (stack.shape[0] - 12) // 2
+        one = centre(stack, first, first + rows)[:, C : 2 * C].astype(f32)
+        grad_one[start : start + rows] = (back * (1.0 - one * one)).astype(bf16)
 
 
 def first_terms(first, grad_one):
@@ -209,9 +219,11 @@
 
 def previous(here, kv_ext, bq, grad_one):
     spread = dot(bq[...], grad_one[...].reshape(12 * C, WIDE))
-    total = 0.0
-    for number, (b, c) in enumerate([(b, c) for b in STEPS for c in STEPS]):
-        total = total + lifted(shifted(spread[number * 16 : number * 16 + 16], -NZ * b), -c)
+    total = here
+    for row, b in enumerate(STEPS):
+        taps = [spread[(row * 3 + i) * 16 : (row * 3 + i + 1) * 16] for i in range(3)]
+        lift = lifted(taps[0], 1) + taps[1] + lifted(taps[2], -1)
+        total = total + shifted(lift, -NZ * b)
     cell = lambda number: kv_ext[number, 4:20, MIDDLE]
     scaled = cell(0) * here
     physics = row_moved(scaled, 1) + row_moved(scaled, -1) - 6.0 * scaled
@@ -220,7 +232,7 @@
     scaled = cell(1) * here
     physics = physics + 0.5 * (row_moved(scaled, 1) - row_moved(scaled, -1))
     physics = physics + central_y(cell(2) * here) + central_z(cell(3) * here)
-    return here + time_step * physics + total
+    return total + time_step * physics
 
 
 def iota(shape, dimension):
@@ -434,7 +446,7 @@
     back_two = dot(bb[...], pair_two)
     grad_two = cotangent_two(back_two, two_two, 0, 14).reshape(14 * C, WIDE)
     z_stack(grad_two, grad_stack, -1, 0)
-    cotangent_one(w_bwd, stack_two, grad_stack, grad_one, (0, 3, 6, 9))
+    cotangent_one(w_bwd, stack_two, grad_stack, grad_one, 0, 12)
     adjoint = previous(g_ext[4:20, :], kv_ext, bq, grad_one)
     a_ext[own] = adjoint[4:12, OWN_LANES]
     tiles.append(send_around(a_ext, sems(3), place))
@@ -466,7 +478,7 @@
     here = a_ext[4:20, :]
     full = cotangent_two(dot(bb[C : 13 * C, :], flux_pair(here)), two_one, 4, 16)
     z_stack(full.reshape(12 * C, WIDE), grad_stack, -1, 1)
-    cotangent_one(w_bwd, stack_one, grad_stack, grad_one, (1, 4, 7, 8))
+    cotangent_one(w_bwd, stack_one, grad_stack, grad_one, 1, 11)
     in_one, bias_in_one = first_terms(first_one, grad_one)
     matrix = jnp.concatenate(
         [in_one + in_two, bias_in_one + bias_in_two]
@@ -504,7 +516,7 @@
     total = recv_y[0]
     for k in range(1, size_y):
         total = total + recv_y[k]
-    gathered[share(me_x), :] = total * scale
+    gathered[share(me_x), :] = (total * scale).astype(bf16)
     for peer in peers_x:
         remote(gathered.at[share(me_x)], gathered.at[share(me_x)], sems(6), peer)
 
@@ -513,14 +525,14 @@
     for k in range(1, size_y):
         total = total + small_y[k]
     out_small[...] = total * scale
-    wait_tiles(recv_sem.at[6], gauge, per * (size_x - 1))
+    wait_tiles(recv_sem.at[6], gauge, per // 2 * (size_x - 1))
     out_sums[...] = gathered[...]
 
     for number in range(4):
         wait_tiles(send_sem.at[number], gauge, tiles[number])
     wait_tiles(send_sem.at[4], gauge, per * (size_x - 1))
     wait_tiles(send_sem.at[5], gauge, per * (size_y - 1))
-    wait_tiles(send_sem.at[6], gauge, per * (size_x - 1))
+    wait_tiles(send_sem.at[6], gauge, per // 2 * (size_x - 1))
     wait_tiles(send_sem.at[7], gauge, size_x - 1)
     wait_tiles(send_sem.at[8], gauge, size_y - 1)
 
@@ -535,7 +547,7 @@
                     value = sums[row : row + C, b * C : (b + 1) * C]
                 else:
                     value = sums[b * C : (b + 1) * C, 3 * C :]
-                out_mid[a * 9 + b * 3 + c] = value
+                out_mid[a * 9 + b * 3 + c] = value.astype(f32)
     for number in range(3):
         out_in[number * 8 : number * 8 + 8] = small[:, number * C : (number + 1) * C]
     last = small[:, 3 * C :]
@@ -560,7 +572,7 @@
         shape = jax.ShapeDtypeStruct
         outs = pl.pallas_call(
             lambda *refs: kernel(size_x, size_y, 1.0 / math.sqrt(cells), *refs),
-            out_shape=[shape((ROWS, LANES), f32), shape((256, 128), f32), shape((8, 128), f32)],
+            out_shape=[shape((ROWS, LANES), f32), shape((256, 128), bf16), shape((8, 128), f32)],
             in_specs=[anywhere] * 9,
             out_specs=[vmem] * 3,
             scratch_shapes=[
@@ -590,7 +602,7 @@
                 pltpu.VMEM((256, 128), f32),
                 pltpu.VMEM((size_x, part, 128), f32),
                 pltpu.VMEM((size_y, part, 128), f32),
-                pltpu.VMEM((256, 128), f32),
+                pltpu.VMEM((256, 128), bf16),
                 pltpu.VMEM((8, 128), f32),
                 pltpu.VMEM((size_x, 8, 128), f32),
                 pltpu.VMEM((size_y, 8, 128), f32),

time: 45.6 us -> 44.9 us (0.985)
  Pallas kernels: 44.8 us -> 44 us
    pallas_call x1, Pallas kernels: 42.9 us -> 42.3 us  [shards(): pl.pallas_call(lambda *refs: kernel(size_x, size_y, 1.0 / math.sqrt(cells...]
where the time goes in v4:
time: 44.9 us; the launch traced here: 44.7 us
  Pallas kernels  44 us (98%)
  between operations  0.64 us (1%)
    pallas_call x1, Pallas kernels, shards(): pl.pallas_call(lambda *refs: kernel(size_x, size_y, 1.0 / math.sqrt(cells...  42.3 us
    pallas_call x1, Pallas kernels, shards(): pl.pallas_call(unpack, out_shape=[shape((ROWS, LANES), f32), shape((27, C...  1.72 us

profile of v4, /device:TPU:1, one launch (start us, length us, event | category | flops | bytes accessed | tf_op | source)
XLA Modules:
  0.0 44.7 jit_solution(8318781401751228142)
XLA Ops:
  0.6 42.3 %shard_map.136 = (f32[8,512]{1,0:T(8,128)}, bf16[256,128]{1,0:T(8,128)(2,1)}, f32[8,128]{1,0:T(8,128)}) custom-call(f32[8,512]{1,0:T(8,128)} %refs_0_.1, f32[8,512]{1,0:T(8,128)} %refs_1_.1, f32[8,512]{1,0:T(8,128)} %refs_2_.1, f32[3,8,512]{2,1,0:T(8,128)} %refs_3_.1, bf16[27,32]{1,0:T(8,128)(2,1)} %refs_4_.1, f32[1,32]{1,0:T(1,128)} %bitcast.7, ...), custom_call_target="tpu_custom_call" | custom-call | tf_op jit(solution)/shard_map/pallas_call | solution.py:573
  43.0 1.7 %shard_map.137 = (f32[8,512]{1,0:T(8,128)}, f32[27,32]{1,0:T(8,128)}, f32[1,32]{1,0:T(1,128)}, f32[27,32,32]{2,1,0:T(8,128)}, f32[1,32]{1,0:T(1,128)}, /*index=5*/f32[3,32]{1,0:T(4,128)}) custom-call(f32[8,512]{1,0:T(8,128)} %get-tuple-element.15.field, bf16[256,128]{1,0:T(8,128)(2,1)} %get-tuple-element.16.sums, f32[8,128]{1,0:T(8,128)} %get-tuple-element.17.small), custom_call_target="tpu_custom_call" | custom-call | tf_op jit(solution)/shard_map/pallas_call | solution.py:621

commit v5 on v4

--- a/solution.py
+++ b/solution.py
@@ -122,7 +122,7 @@
 
 
 def stepped(field_ext, kv_ext, bf, hidden_two):
-    flux = dot(bf[...], hidden_two[...].reshape(20 * C, BROAD))
+    flux = dot(bf[...], hidden_two[...].reshape(18 * C, BROAD))
     correction = flux[0:TALL] + central_y(flux[TALL : 2 * TALL]) + central_z(flux[2 * TALL :])
     here = field_ext[...]
     up, down = row_moved(here, 1), row_moved(here, -1)
@@ -162,46 +162,48 @@
     return ref[low:high, :, margin : margin + WIDE]
 
 
-def middle_terms(stack, own_two, spread):
-    first_row = (stack.shape[0] - ROWS) // 2 - 1
-    own = own_lanes_only(own_two.astype(f32))
+def middle_terms(stack, values, spread):
+    rows = values.shape[0] // C
+    first_row = (stack.shape[0] - rows) // 2 - 1
+    wide = values.astype(f32)
     for number, b in enumerate(STEPS):
-        moved = shifted(own, -NZ * b).astype(bf16)
-        spread[:, number * C : (number + 1) * C, :] = moved.reshape(8, C, WIDE)
+        moved = shifted(wide, -NZ * b).astype(bf16) if b else values
+        spread[0:rows, number * C : (number + 1) * C, :] = moved.reshape(rows, C, WIDE)
     pairs = jnp.zeros((12 * C, 6 * C), f32)
-    for x in range(0, ROWS, 2):
+    for x in range(0, rows, 2):
         window = centre(stack, first_row + x, first_row + x + 4).reshape(12 * C, WIDE)
         pairs = pairs + dot_lanes(window, spread[x : x + 2].reshape(6 * C, WIDE))
-    term_mid = pairs[0 : 9 * C, 0 : 3 * C] + pairs[3 * C :, 3 * C :]
-    return term_mid
-
-
-def out_terms(pair, hidden_two, own_two):
-    own = own_lanes_only(own_two.astype(f32))
-    bias_mid = jnp.sum(jnp.sum(own.reshape(8, C, WIDE), axis=0), axis=1, keepdims=True)
-    masked = own_lanes_only(pair.astype(f32)).astype(bf16)
-    first_row = (hidden_two.shape[0] - ROWS) // 2
-    two = centre(hidden_two, first_row, first_row + ROWS)
-    outer = dot_lanes(two.reshape(8 * C, WIDE), masked)
+    return pairs[0 : 9 * C, 0 : 3 * C] + pairs[3 * C :, 3 * C :]
+
+
+def channel_sums(values):
+    wide = values.astype(f32).reshape(values.shape[0] // C, C, WIDE)
+    return column_to_row(jnp.sum(jnp.sum(wide, axis=0), axis=1, keepdims=True))
+
+
+def out_terms(pair, hidden_two, rows):
+    first_row = (hidden_two.shape[0] - rows) // 2
+    two = centre(hidden_two, first_row, first_row + rows)
+    outer = dot_lanes(two.reshape(rows * C, WIDE), pair)
     row_x = lax.broadcasted_iota(jnp.int32, outer.shape, 0) // C
     col = lax.broadcasted_iota(jnp.int32, outer.shape, 1)
-    outer = jnp.where(col % 16 == row_x + 4, outer, 0.0)
-    outer = jnp.sum(outer.reshape(8, C, outer.shape[1]), axis=0)
+    outer = jnp.where(col % 16 == row_x + 8 - rows // 2, outer, 0.0)
+    outer = jnp.sum(outer.reshape(rows, C, outer.shape[1]), axis=0)
     kind = (lax.broadcasted_iota(jnp.int32, outer.shape, 1) // 16) % 3
     columns = [jnp.sum(jnp.where(kind == d, outer, 0.0), axis=1, keepdims=True) for d in range(3)]
-    return [column_to_row(column) for column in [bias_mid] + columns]
-
-
-def cotangent_one(w_bwd, stack, grad_stack, grad_one, low, high):
-    for start, rows in groups(low, high):
+    return [column_to_row(column) for column in columns]
+
+
+def cotangent_one(w_bwd, stack, grad_stack, grad_one):
+    for start, rows in groups(0, 10):
         back = middle_conv(w_bwd, grad_stack, start, rows, -1)
-        first = start + (stack.shape[0] - 12) // 2
+        first = start + (stack.shape[0] - 10) // 2
         one = centre(stack, first, first + rows)[:, C : 2 * C].astype(f32)
         grad_one[start : start + rows] = (back * (1.0 - one * one)).astype(bf16)
 
 
 def first_terms(first, grad_one):
-    own = own_lanes_only(grad_one[2:10].reshape(8 * C, WIDE).astype(f32))
+    own = own_lanes_only(grad_one[1:9].reshape(8 * C, WIDE).astype(f32))
     outer = dot_lanes(first, own.astype(bf16))
     row_x = lax.broadcasted_iota(jnp.int32, outer.shape, 0) % TALL
     col_x = lax.broadcasted_iota(jnp.int32, outer.shape, 1) // C
@@ -213,12 +215,11 @@
     folded = folded[:, :128] + folded[:, 128:]
     folded = folded + pltpu.roll(folded, 64, axis=1)
     folded = folded + pltpu.roll(folded, 32, axis=1)
-    bias_in = jnp.sum(jnp.sum(own.reshape(8, C, WIDE), axis=0), axis=1, keepdims=True)
-    return folded[:, :C], column_to_row(bias_in)
+    return folded[:, :C], channel_sums(own)
 
 
 def previous(here, kv_ext, bq, grad_one):
-    spread = dot(bq[...], grad_one[...].reshape(12 * C, WIDE))
+    spread = dot(bq[...], grad_one[...].reshape(10 * C, WIDE))
     total = here
     for row, b in enumerate(STEPS):
         taps = [spread[(row * 3 + i) * 16 : (row * 3 + i + 1) * 16] for i in range(3)]
@@ -274,27 +275,27 @@
     for i in range(22):
         rows = sum(jnp.where(j == i + a, spread[a], 0.0) for a in range(3))
         b0[i * C : (i + 1) * C, :] = rows.astype(bf16)
-    shape = (C, 12 * C)
+    shape = (C, 10 * C)
     tiled = dot(taps, ones_where(iota(shape, 1) % C == iota(shape, 0))).astype(bf16)
     total = 0.0
     for a in range(3):
         pick = ones_where(iota((144, 27), 1) == iota((144, 27), 0) // 16 + 9 * a)
         rows = dot(pick, tiled)
-        kept = iota(rows.shape, 1) // C == iota(rows.shape, 0) % 16 - a - 1
+        kept = iota(rows.shape, 1) // C == iota(rows.shape, 0) % 16 - a - 2
         total = total + jnp.where(kept, rows, 0.0)
     bq[...] = total.astype(bf16)
 
 
 def place_flux(flux, bf, bb):
     taps = flux[...]
-    shape = (C, 20 * C)
+    shape = (C, 18 * C)
     tiled = dot(taps, ones_where(iota(shape, 1) % C == iota(shape, 0))).astype(bf16)
     shape = (3 * TALL, 3)
     rows = dot(ones_where(iota(shape, 1) == iota(shape, 0) // TALL), tiled)
     x, i = iota(rows.shape, 0) % TALL, iota(rows.shape, 1) // C
     first = iota(rows.shape, 0) < TALL
-    factor = jnp.where(i == x - 1, 0.5, jnp.where(i == x - 3, -0.5, 0.0))
-    factor = jnp.where(first, factor, jnp.where(i == x - 2, 1.0, 0.0))
+    factor = jnp.where(i == x - 2, 0.5, jnp.where(i == x - 4, -0.5, 0.0))
+    factor = jnp.where(first, factor, jnp.where(i == x - 3, 1.0, 0.0))
     bf[...] = (rows * factor).astype(bf16)
     pick = ones_where(iota((3, 96), 0) == (iota((3, 96), 1) // 16) % 3)
     columns = dot_rows(taps, pick)
@@ -434,28 +435,30 @@
     weights = (b0, bias_in, w_fwd, bias_mid)
     wait_tiles(recv_sem.at[0], gauge, tiles[0])
     first_one = first_stack(f_ext)
-    forward(first_one, 0, weights, stack_one, two_one)
+    forward(first_one, 1, weights, stack_one, two_one)
     first_one = first_one[:, MIDDLE]
     wait_tiles(recv_sem.at[1], gauge, tiles[1])
     f1_ext[...] = stepped(f_ext, kv_ext, bf, two_one)
     first_two = first_stack(f1_ext)[:, MIDDLE]
-    forward(first_two, 3, weights, stack_two, two_two)
+    forward(first_two, 4, weights, stack_two, two_two)
 
     wait_tiles(recv_sem.at[2], gauge, tiles[2])
     pair_two = flux_pair(g_ext[4:20, :])
-    back_two = dot(bb[...], pair_two)
-    grad_two = cotangent_two(back_two, two_two, 0, 14).reshape(14 * C, WIDE)
+    back_two = dot(bb[C : 13 * C, :], pair_two)
+    grad_two = cotangent_two(back_two, two_two, 0, 12).reshape(12 * C, WIDE)
     z_stack(grad_two, grad_stack, -1, 0)
-    cotangent_one(w_bwd, stack_two, grad_stack, grad_one, 0, 12)
+    cotangent_one(w_bwd, stack_two, grad_stack, grad_one)
     adjoint = previous(g_ext[4:20, :], kv_ext, bq, grad_one)
     a_ext[own] = adjoint[4:12, OWN_LANES]
     tiles.append(send_around(a_ext, sems(3), place))
 
-    own_two = grad_two[3 * C : 11 * C]
+    own_two = own_lanes_only(grad_two[2 * C : 10 * C].astype(f32)).astype(bf16)
     mid = middle_terms(stack_two, own_two, spread)
-    pair_one = flux_pair(adjoint)
-    own_one = cotangent_two(dot(bb[3 * C : 11 * C, :], pair_one), two_one, 6, 14)
-    own_one = own_one.reshape(8 * C, WIDE)
+    row = lax.broadcasted_iota(jnp.int32, adjoint.shape, 0)
+    share_one = own_lanes_only(jnp.where((row >= 4) & (row < 12), adjoint, 0.0))
+    pair_one = flux_pair(share_one)
+    back_one = dot(bb[2 * C : 12 * C, :], pair_one)
+    own_one = cotangent_two(back_one, two_one, 4, 14).reshape(10 * C, WIDE)
     mid = mid + middle_terms(stack_one, own_one, spread)
     sums[:, 0 : 3 * C] = mid[0 : 8 * C]
     for number in range(3):
@@ -472,13 +475,16 @@
         remote(sums.at[share(peer[0])], recv_x.at[me_x], sems(4), peer)
 
     in_two, bias_in_two = first_terms(first_two, grad_one)
-    rows_two = out_terms(pair_two, two_two, own_two)
-    rows_one = out_terms(pair_one, two_one, own_one)
+    pair_two = own_lanes_only(pair_two.astype(f32)).astype(bf16)
+    rows_two = [channel_sums(own_two)] + out_terms(pair_two, two_two, 8)
+    rows_one = out_terms(pair_one, two_one, 10)
     wait_tiles(recv_sem.at[3], gauge, tiles[3])
     here = a_ext[4:20, :]
-    full = cotangent_two(dot(bb[C : 13 * C, :], flux_pair(here)), two_one, 4, 16)
-    z_stack(full.reshape(12 * C, WIDE), grad_stack, -1, 1)
-    cotangent_one(w_bwd, stack_one, grad_stack, grad_one, 1, 11)
+    full = cotangent_two(dot(bb[C : 13 * C, :], flux_pair(here)), two_one, 3, 15)
+    full = full.reshape(12 * C, WIDE)
+    z_stack(full, grad_stack, -1, 0)
+    rows_one = [channel_sums(own_lanes_only(full[2 * C : 10 * C].astype(f32)))] + rows_one
+    cotangent_one(w_bwd, stack_one, grad_stack, grad_one)
     in_one, bias_in_one = first_terms(first_one, grad_one)
     matrix = jnp.concatenate(
         [in_one + in_two, bias_in_one + bias_in_two]
@@ -588,17 +594,17 @@
                 pltpu.VMEM((288, 480), f32),
                 pltpu.VMEM((22 * C, 9 * TALL), bf16),
                 pltpu.VMEM((288, 480), bf16),
-                pltpu.VMEM((3 * TALL, 20 * C), bf16),
+                pltpu.VMEM((3 * TALL, 18 * C), bf16),
                 pltpu.VMEM((14 * C, 96), bf16),
                 pltpu.VMEM((288, 480), bf16),
-                pltpu.VMEM((144, 12 * C), bf16),
-                pltpu.VMEM((22, 3 * C, BROAD), bf16),
-                pltpu.VMEM((16, 3 * C, WIDE), bf16),
-                pltpu.VMEM((20, C, BROAD), bf16),
-                pltpu.VMEM((14, C, WIDE), bf16),
-                pltpu.VMEM((8, 3 * C, WIDE), bf16),
+                pltpu.VMEM((144, 10 * C), bf16),
+                pltpu.VMEM((20, 3 * C, BROAD), bf16),
                 pltpu.VMEM((14, 3 * C, WIDE), bf16),
+                pltpu.VMEM((18, C, BROAD), bf16),
                 pltpu.VMEM((12, C, WIDE), bf16),
+                pltpu.VMEM((10, 3 * C, WIDE), bf16),
+                pltpu.VMEM((12, 3 * C, WIDE), bf16),
+                pltpu.VMEM((10, C, WIDE), bf16),
                 pltpu.VMEM((256, 128), f32),
                 pltpu.VMEM((size_x, part, 128), f32),
                 pltpu.VMEM((size_y, part, 128), f32),

time: 44.9 us -> 44.1 us (0.982)
  Pallas kernels: 44 us -> 43.3 us
    pallas_call x1, Pallas kernels: 42.3 us -> 41.6 us  [shards(): pl.pallas_call(lambda *refs: kernel(size_x, size_y, 1.0 / math.sqrt(cells...]
where the time goes in v5:
time: 44.1 us; the launch traced here: 44 us
  Pallas kernels  43.3 us (98%)
  between operations  0.64 us (1%)
    pallas_call x1, Pallas kernels, shards(): pl.pallas_call(lambda *refs: kernel(size_x, size_y, 1.0 / math.sqrt(cells...  41.6 us
    pallas_call x1, Pallas kernels, shards(): pl.pallas_call(unpack, out_shape=[shape((ROWS, LANES), f32), shape((27, C...  1.72 us

profile of v5, /device:TPU:1, one launch (start us, length us, event | category | flops | bytes accessed | tf_op | source)
XLA Modules:
  0.0 44.0 jit_solution(15434670373934082841)
XLA Ops:
  0.6 41.6 %shard_map.136 = (f32[8,512]{1,0:T(8,128)}, bf16[256,128]{1,0:T(8,128)(2,1)}, f32[8,128]{1,0:T(8,128)}) custom-call(f32[8,512]{1,0:T(8,128)} %refs_0_.1, f32[8,512]{1,0:T(8,128)} %refs_1_.1, f32[8,512]{1,0:T(8,128)} %refs_2_.1, f32[3,8,512]{2,1,0:T(8,128)} %refs_3_.1, bf16[27,32]{1,0:T(8,128)(2,1)} %refs_4_.1, f32[1,32]{1,0:T(1,128)} %bitcast.7, ...), custom_call_target="tpu_custom_call" | custom-call | tf_op jit(solution)/shard_map/pallas_call | solution.py:579
  42.3 1.7 %shard_map.137 = (f32[8,512]{1,0:T(8,128)}, f32[27,32]{1,0:T(8,128)}, f32[1,32]{1,0:T(1,128)}, f32[27,32,32]{2,1,0:T(8,128)}, f32[1,32]{1,0:T(1,128)}, /*index=5*/f32[3,32]{1,0:T(4,128)}) custom-call(f32[8,512]{1,0:T(8,128)} %get-tuple-element.15.field, bf16[256,128]{1,0:T(8,128)(2,1)} %get-tuple-element.16.sums, f32[8,128]{1,0:T(8,128)} %get-tuple-element.17.small), custom_call_target="tpu_custom_call" | custom-call | tf_op jit(solution)/shard_map/pallas_call | solution.py:627

commit v6 on v5

--- a/solution.py
+++ b/solution.py
@@ -125,15 +125,15 @@
     flux = dot(bf[...], hidden_two[...].reshape(18 * C, BROAD))
     correction = flux[0:TALL] + central_y(flux[TALL : 2 * TALL]) + central_z(flux[2 * TALL :])
     here = field_ext[...]
+    y_up, y_down = shifted(here, NZ)[:, MIDDLE], shifted(here, -NZ)[:, MIDDLE]
+    here = here[:, MIDDLE]
     up, down = row_moved(here, 1), row_moved(here, -1)
-    laplace = (
-        up + down + shifted(here, NZ) + shifted(here, -NZ) + lifted(here, 1) + lifted(here, -1)
-    )
+    laplace = up + down + y_up + y_down + lifted(here, 1) + lifted(here, -1)
     physics = kv_ext[0] * (laplace - 6.0 * here)
     physics = physics - kv_ext[1] * (0.5 * (up - down))
-    physics = physics - kv_ext[2] * central_y(here)
+    physics = physics - kv_ext[2] * (0.5 * (y_up - y_down))
     physics = physics - kv_ext[3] * central_z(here)
-    return here + time_step * (physics + correction)
+    return here + time_step * (physics + correction[:, MIDDLE])
 
 
 def row_moved(values, count):
@@ -225,7 +225,7 @@
         taps = [spread[(row * 3 + i) * 16 : (row * 3 + i + 1) * 16] for i in range(3)]
         lift = lifted(taps[0], 1) + taps[1] + lifted(taps[2], -1)
         total = total + shifted(lift, -NZ * b)
-    cell = lambda number: kv_ext[number, 4:20, MIDDLE]
+    cell = lambda number: kv_ext[number, 4:20, :]
     scaled = cell(0) * here
     physics = row_moved(scaled, 1) + row_moved(scaled, -1) - 6.0 * scaled
     physics = physics + shifted(scaled, NZ) + shifted(scaled, -NZ)
@@ -326,7 +326,7 @@
     copy.start()
 
 
-def send_around(ext, sems, place):
+def send_around(ext, sems, place, block=None):
     (me_x, size_x), (me_y, size_y) = place
     width = ext.shape[-1]
     side = (width - LANES) // 2
@@ -340,6 +340,9 @@
             lax.rem(me_y + dy + size_y, size_y),
         )
         source = ext.at[lead + (OWN_ROWS, sources[dy])]
+        if block is not None:
+            lanes = sources[dy]
+            source = block.at[:, pl.ds(lanes.start - side, lanes.stop - lanes.start)]
         remote(source, ext.at[lead + (rows[dx], targets[dy])], sems, peer)
     depth = ext.shape[0] if lead else 1
     return depth * (3 * width - LANES) // 128
@@ -407,8 +410,8 @@
     for source, target in (
         (field, f_ext.at[broad_own]),
         (cotangent, g_ext.at[own]),
-        (kappa, kv_ext.at[(0,) + broad_own]),
-        (vel, kv_ext.at[(slice(1, 4),) + broad_own]),
+        (kappa, kv_ext.at[(0,) + own]),
+        (vel, kv_ext.at[(slice(1, 4),) + own]),
         (conv_in_in, conv_in),
         (bias_in_in, bias_in_row),
         (conv_mid_in, conv_mid),
@@ -418,13 +421,12 @@
         copy = pltpu.make_async_copy(source, target, local_sem.at[len(arrivals)])
         copy.start()
         arrivals.append(copy)
+    sems = lambda number: (send_sem.at[number], recv_sem.at[number])
+    pl.semaphore_wait(barrier, len(near + peers_x + peers_y))
+    tiles = [send_around(f_ext, sems(0), place, field)]
     for copy in arrivals:
         copy.wait()
-    sems = lambda number: (send_sem.at[number], recv_sem.at[number])
-    pl.semaphore_wait(barrier, len(near + peers_x + peers_y))
-    tiles = [
-        send_around(ext, sems(number), place) for number, ext in enumerate((f_ext, kv_ext, g_ext))
-    ]
+    tiles += [send_around(kv_ext, sems(1), place), send_around(g_ext, sems(2), place)]
 
     bias_in[...] = row_to_column(bias_in_row[...])
     bias_mid[...] = row_to_column(bias_mid_row[...])
@@ -439,7 +441,7 @@
     first_one = first_one[:, MIDDLE]
     wait_tiles(recv_sem.at[1], gauge, tiles[1])
     f1_ext[...] = stepped(f_ext, kv_ext, bf, two_one)
-    first_two = first_stack(f1_ext)[:, MIDDLE]
+    first_two = first_stack(f1_ext)
     forward(first_two, 4, weights, stack_two, two_two)
 
     wait_tiles(recv_sem.at[2], gauge, tiles[2])
@@ -450,10 +452,10 @@
     cotangent_one(w_bwd, stack_two, grad_stack, grad_one)
     adjoint = previous(g_ext[4:20, :], kv_ext, bq, grad_one)
     a_ext[own] = adjoint[4:12, OWN_LANES]
-    tiles.append(send_around(a_ext, sems(3), place))
 
     own_two = own_lanes_only(grad_two[2 * C : 10 * C].astype(f32)).astype(bf16)
     mid = middle_terms(stack_two, own_two, spread)
+    tiles.append(send_around(a_ext, sems(3), place))
     row = lax.broadcasted_iota(jnp.int32, adjoint.shape, 0)
     share_one = own_lanes_only(jnp.where((row >= 4) & (row < 12), adjoint, 0.0))
     pair_one = flux_pair(share_one)
@@ -582,8 +584,8 @@
             in_specs=[anywhere] * 9,
             out_specs=[vmem] * 3,
             scratch_shapes=[
-                broad, broad, ext, ext,
-                pltpu.VMEM((4, TALL, BROAD), f32),
+                broad, ext, ext, ext,
+                pltpu.VMEM((4, TALL, WIDE), f32),
                 pltpu.VMEM((27, C), bf16),
                 pltpu.VMEM((1, C), f32),
                 pltpu.VMEM((27, C, C), bf16),

time: 44.1 us -> 43.9 us (level)
  no operation moved by 1% of the time
where the time goes in v6:
time: 43.9 us; the launch traced here: 43.8 us
  Pallas kernels  43.1 us (98%)
  between operations  0.64 us (1%)
    pallas_call x1, Pallas kernels, shards(): pl.pallas_call(lambda *refs: kernel(size_x, size_y, 1.0 / math.sqrt(cells...  41.4 us
    pallas_call x1, Pallas kernels, shards(): pl.pallas_call(unpack, out_shape=[shape((ROWS, LANES), f32), shape((27, C...  1.72 us

profile of v6, /device:TPU:1, one launch (start us, length us, event | category | flops | bytes accessed | tf_op | source)
XLA Modules:
  0.0 43.8 jit_solution(8961105568545673199)
XLA Ops:
  0.6 41.4 %shard_map.136 = (f32[8,512]{1,0:T(8,128)}, bf16[256,128]{1,0:T(8,128)(2,1)}, f32[8,128]{1,0:T(8,128)}) custom-call(f32[8,512]{1,0:T(8,128)} %refs_0_.1, f32[8,512]{1,0:T(8,128)} %refs_1_.1, f32[8,512]{1,0:T(8,128)} %refs_2_.1, f32[3,8,512]{2,1,0:T(8,128)} %refs_3_.1, bf16[27,32]{1,0:T(8,128)(2,1)} %refs_4_.1, f32[1,32]{1,0:T(1,128)} %bitcast.7, ...), custom_call_target="tpu_custom_call" | custom-call | tf_op jit(solution)/shard_map/pallas_call | solution.py:581
  42.0 1.7 %shard_map.137 = (f32[8,512]{1,0:T(8,128)}, f32[27,32]{1,0:T(8,128)}, f32[1,32]{1,0:T(1,128)}, f32[27,32,32]{2,1,0:T(8,128)}, f32[1,32]{1,0:T(1,128)}, /*index=5*/f32[3,32]{1,0:T(4,128)}) custom-call(f32[8,512]{1,0:T(8,128)} %get-tuple-element.15.field, bf16[256,128]{1,0:T(8,128)(2,1)} %get-tuple-element.16.sums, f32[8,128]{1,0:T(8,128)} %get-tuple-element.17.small), custom_call_target="tpu_custom_call" | custom-call | tf_op jit(solution)/shard_map/pallas_call | solution.py:629

commit v7 on v6

--- a/solution.py
+++ b/solution.py
@@ -388,7 +388,7 @@
     f_ext, f1_ext, g_ext, a_ext, kv_ext, conv_in, bias_in_row, conv_mid, bias_mid_row, flux,
     bias_in, bias_mid, wide, b0, w_fwd, bf, bb, w_bwd, bq,
     stack_one, stack_two, two_one, two_two, spread, grad_stack, grad_one,
-    sums, recv_x, recv_y, gathered, small, small_x, small_y, gauge,
+    sums, recv_x, recv_y, gathered, small, small_x, small_y, last_field, last_small, gauge,
     local_sem, send_sem, recv_sem,
 ):
     me_x, me_y = lax.axis_index("gx"), lax.axis_index("gy")
@@ -510,7 +510,9 @@
         remote(small, small_x.at[me_x], sems(7), peer)
 
     final = previous(here, kv_ext, bq, grad_one)
-    out_field[...] = final[4:12, OWN_LANES]
+    last_field[...] = final[4:12, OWN_LANES]
+    results = [pltpu.make_async_copy(last_field, out_field, local_sem.at[0])]
+    results[0].start()
 
     wait_tiles(recv_sem.at[7], gauge, size_x - 1)
     total = small_x[0]
@@ -532,9 +534,12 @@
     total = small_y[0]
     for k in range(1, size_y):
         total = total + small_y[k]
-    out_small[...] = total * scale
+    last_small[...] = total * scale
+    results.append(pltpu.make_async_copy(last_small, out_small, local_sem.at[1]))
+    results[1].start()
     wait_tiles(recv_sem.at[6], gauge, per // 2 * (size_x - 1))
-    out_sums[...] = gathered[...]
+    results.append(pltpu.make_async_copy(gathered, out_sums, local_sem.at[2]))
+    results[2].start()
 
     for number in range(4):
         wait_tiles(send_sem.at[number], gauge, tiles[number])
@@ -543,6 +548,8 @@
     wait_tiles(send_sem.at[6], gauge, per // 2 * (size_x - 1))
     wait_tiles(send_sem.at[7], gauge, size_x - 1)
     wait_tiles(send_sem.at[8], gauge, size_y - 1)
+    for copy in results:
+        copy.wait()
 
 
 def unpack(field, sums, small, out_field, out_in, out_bias_in, out_mid, out_bias_mid, out_out):
@@ -582,7 +589,7 @@
             lambda *refs: kernel(size_x, size_y, 1.0 / math.sqrt(cells), *refs),
             out_shape=[shape((ROWS, LANES), f32), shape((256, 128), bf16), shape((8, 128), f32)],
             in_specs=[anywhere] * 9,
-            out_specs=[vmem] * 3,
+            out_specs=[anywhere] * 3,
             scratch_shapes=[
                 broad, ext, ext, ext,
                 pltpu.VMEM((4, TALL, WIDE), f32),
@@ -614,6 +621,8 @@
                 pltpu.VMEM((8, 128), f32),
                 pltpu.VMEM((size_x, 8, 128), f32),
                 pltpu.VMEM((size_y, 8, 128), f32),
+                pltpu.VMEM((ROWS, LANES), f32),
+                pltpu.VMEM((8, 128), f32),
                 pltpu.VMEM((640, 128), f32),
                 pltpu.SemaphoreType.DMA((9,)),
                 pltpu.SemaphoreType.DMA((9,)),

time: 43.9 us -> 43.9 us (level)
  no operation moved by 1% of the time
where the time goes in v7:
time: 43.9 us; the launch traced here: 43.7 us
  Pallas kernels  43.1 us (98%)
  between operations  0.64 us (1%)
    pallas_call x1, Pallas kernels, shards(): pl.pallas_call(lambda *refs: kernel(size_x, size_y, 1.0 / math.sqrt(cells...  41.4 us
    pallas_call x1, Pallas kernels, shards(): pl.pallas_call(unpack, out_shape=[shape((ROWS, LANES), f32), shape((27, C...  1.72 us

profile of v7, /device:TPU:1, one launch (start us, length us, event | category | flops | bytes accessed | tf_op | source)
XLA Modules:
  0.0 43.7 jit_solution(16343770937432216176)
XLA Ops:
  0.6 41.4 %shard_map.136 = (f32[8,512]{1,0:T(8,128)}, bf16[256,128]{1,0:T(8,128)(2,1)}, f32[8,128]{1,0:T(8,128)}) custom-call(f32[8,512]{1,0:T(8,128)} %refs_0_.1, f32[8,512]{1,0:T(8,128)} %refs_1_.1, f32[8,512]{1,0:T(8,128)} %refs_2_.1, f32[3,8,512]{2,1,0:T(8,128)} %refs_3_.1, bf16[27,32]{1,0:T(8,128)(2,1)} %refs_4_.1, f32[1,32]{1,0:T(1,128)} %bitcast.7, ...), custom_call_target="tpu_custom_call" | custom-call | tf_op jit(solution)/shard_map/pallas_call | solution.py:588
  42.0 1.7 %shard_map.137 = (f32[8,512]{1,0:T(8,128)}, f32[27,32]{1,0:T(8,128)}, f32[1,32]{1,0:T(1,128)}, f32[27,32,32]{2,1,0:T(8,128)}, f32[1,32]{1,0:T(1,128)}, /*index=5*/f32[3,32]{1,0:T(4,128)}) custom-call(f32[8,512]{1,0:T(8,128)} %get-tuple-element.15.field, bf16[256,128]{1,0:T(8,128)(2,1)} %get-tuple-element.16.sums, f32[8,128]{1,0:T(8,128)} %get-tuple-element.17.small), custom_call_target="tpu_custom_call" | custom-call | tf_op jit(solution)/shard_map/pallas_call | solution.py:638
